TPU v7x, 256 devices: a whole 4x4x8 slice. The times are simulated.
256 devices in a mesh: tm: 32 (over x, y, core), group: 8 (over z).
Axes of the slice: x: 4, y: 4, z: 8, core: 2. Of those that a mesh axis runs over, the one named last changes fastest.
Arguments:
- frames: bfloat16 [8, 262144, 512], P('group', 'tm')
- pair_count: int32 [8], P('group'), may hold values from 131072 to 260096, as said below
Outputs:
- group_instant: float32 [8, 512, 512], P('group', 'tm')
- group_lagged: float32 [8, 512, 512], P('group', 'tm')
- pooled_instant: float32 [512, 512], P('tm')
- pooled_lagged: float32 [512, 512], P('tm')
Inputs may be any that keep to these rules, and one draw needn't show every extreme that they name: `pair_count`: every session has between 131072 and 260096 pairs, and some session has exactly 260096.
All inputs are finite; a program needn't handle non-finite values.
Results may differ from a plain program's by a relative error of at most 0.0003.
Values may be sent and summed in bfloat16 or wider, within the bound.
No kernel may reach another device: no remote copies, remote signals or barrier semaphores. Data moves between devices by JAX's collectives and lax.ppermute only.
A program may use at most 64 MiB of HBM per device.

v0:
```python
import jax
import jax.numpy as jnp
from jax import lax
from jax.sharding import PartitionSpec as P

LAG = 2048


def passed_along(block, axis, distance):
    devices = range(lax.axis_size(axis))
    route = [(i - distance, i) for i in devices if i - distance in devices]
    return lax.ppermute(block, axis, route)


def on_device(frames, pair_count):
    local = frames[0]
    rows = local.shape[0]
    width = local.shape[1]
    share = width // lax.axis_size("tm")
    count = pair_count[0]
    number = count.astype(jnp.float32)
    position = lax.axis_index("tm") * rows + lax.iota(jnp.int32, rows)
    weight = (position < count).astype(jnp.float32)[:, None]
    incoming = passed_along(local[:LAG], "tm", -1)
    lagged = jnp.concatenate([local[LAG:], incoming], axis=0)
    wide = local.astype(jnp.float32)
    later = lagged.astype(jnp.float32)
    sum_x = jnp.sum(wide * weight, axis=0)
    sum_y = jnp.sum(later * weight, axis=0)
    first_row = lax.axis_index("tm") * share
    contract = (((0,), (0,)), ((), ()))
    tot_x, tot_y = lax.psum((sum_x, sum_y), "tm")
    mean_x = tot_x / number
    mean_y = tot_y / number
    cent_x = (wide - mean_x[None]) * weight
    cent_y = (later - mean_y[None]) * weight
    inst = lax.dot_general(
        cent_x,
        cent_x,
        contract,
        precision=lax.Precision.HIGHEST,
        preferred_element_type=jnp.float32,
    )
    lagm = lax.dot_general(
        cent_x,
        cent_y,
        contract,
        precision=lax.Precision.HIGHEST,
        preferred_element_type=jnp.float32,
    )
    inst_rows, lag_rows = (
        lax.psum_scatter(inst, "tm", scatter_dimension=0, tiled=True),
        lax.psum_scatter(lagm, "tm", scatter_dimension=0, tiled=True),
    )
    mean_rows = lax.dynamic_slice_in_dim(mean_x, first_row, share)
    group_instant = (inst_rows / number)[None]
    group_lagged = (lag_rows / number)[None]
    part_inst = inst_rows + number * mean_rows[:, None] * mean_x[None]
    part_lag = lag_rows + number * mean_rows[:, None] * mean_y[None]
    all_inst, all_lag, all_x, all_y, total = lax.psum(
        (part_inst, part_lag, tot_x, tot_y, number.reshape(1)), "group"
    )
    grand = total[0]
    glob_x = all_x / grand
    glob_y = all_y / grand
    glob_rows = lax.dynamic_slice_in_dim(glob_x, first_row, share)
    pooled_instant = (all_inst - grand * glob_rows[:, None] * glob_x[None]) / grand
    pooled_lagged = (all_lag - grand * glob_rows[:, None] * glob_y[None]) / grand
    return (group_instant, group_lagged, pooled_instant, pooled_lagged)


def solution(mesh):
    in_specs = (P("group", "tm", None), P("group"))
    out_specs = (P("group", "tm", None), P("group", "tm", None), P("tm", None), P("tm", None))
    return jax.shard_map(
        on_device, mesh=mesh, in_specs=in_specs, out_specs=out_specs, check_vma=False
    )
```

profile of v0, /device:TPU:6, one launch (start us, length us, event | category | flops | bytes accessed | tf_op | source)
XLA Modules:
  0.0 364.6 jit_solution(13665067257482250265)
XLA Ops:
  7.2 0.0 reduce-scatter.5.cloned.1.call-start
  7.2 3.1 slice_bitcast_fusion.1
  10.3 4.6 %collective-permute-start = (bf16[2048,512]{1,0:T(8,128)(2,1)}, bf16[2048,512]{1,0:T(8,128)(2,1)S(1)}, u32[]{:S(2)}, u32[]{:S(2)}) collective-permute-start(bf16[2048,512]{1,0:T(8,128)(2,1)} %slice_bitcast_fusion.1), channel_id=1, source_target_pairs={{8,0},{16,8},{24,16},{32,24},{40,32},{48,40},{56,48},{64,56},{72,6... | collective-permute-start | bytes 6291464 | tf_op jit(solution)/shard_map/ppermute | solution.py:12
  15.6 0.0 copy-start
  15.6 3.4 slice_bitcast_fusion
  19.0 0.0 copy-start.1
  19.0 19.8 %collective-permute-done = bf16[2048,512]{1,0:T(8,128)(2,1)S(1)} collective-permute-done((bf16[2048,512]{1,0:T(8,128)(2,1)}, bf16[2048,512]{1,0:T(8,128)(2,1)S(1)}, u32[]{:S(2)}, u32[]{:S(2)}) %collective-permute-start) | collective-permute-done | bytes 2097184 | tf_op jit(solution)/shard_map/ppermute | solution.py:12
  38.8 0.0 copy-done
  38.8 11.3 %fusion.10 = (f32[512]{0:T(512)S(1)}, f32[512]{0:T(512)S(1)}) fusion(f32[8192]{0:T(1024)S(1)} %fusion.18, bf16[2048,512]{1,0:T(8,128)(2,1)S(1)} %collective-permute-done, bf16[6144,512]{1,0:T(8,128)(2,1)S(1)} %slice_bitcast_fusion, bf16[1,8192,512]{2,1,0:T(8,128)(2,1)S(1)} %copy-done), kind=kLoop, calls=%fused_computation.12 | loop fusion | flops 37747712 | bytes 16814080 | tf_op jit(solution)/shard_map/reduce_sum | solution.py:29
  50.0 0.0 copy-done.1
  50.0 56.9 %all-reduce = (f32[512]{0:T(512)S(1)}, f32[512]{0:T(512)S(1)}) all-reduce(f32[512]{0:T(512)S(1)} %get-tuple-element.5, f32[512]{0:T(512)S(1)} %get-tuple-element.4), channel_id=1, replica_groups=mesh['tm'=32,'group'=8] {'tm'}, use_global_device_ids=true, to_apply=%region_1.0 | all-reduce | flops 1024 | bytes 8192 | tf_op jit(solution)/shard_map/psum | solution.py:32
  106.9 38.4 %fusion.4 = f32[512,512]{1,0:T(8,128)} fusion(bf16[1,8192,512]{2,1,0:T(8,128)(2,1)} %param.2, f32[512]{0:T(512)S(1)} %broadcast_divide_fusion.2, f32[512]{0:T(512)S(1)} %broadcast_divide_fusion.3, f32[8192]{0:T(1024)S(1)} %fusion.18, bf16[2048,512]{1,0:T(8,128)(2,1)S(1)} %collective-permute-done, bf16[6144,512]{1,0:T(8,128)(2,1)} %copy-done.1), kind=kOutput, calls=%fused_computation.8 | convolution fusion | flops 25807552512 | bytes 17862656 | tf_op jit(solution)/shard_map/dot_general | solution.py:44
  145.3 0.0 reduce-scatter.5.cloned.1.call-update
  145.3 0.2 reduce-scatter.3.cloned.1.call-start
  145.6 36.6 %fusion.8 = f32[512,512]{1,0:T(8,128)} fusion(bf16[1,8192,512]{2,1,0:T(8,128)(2,1)} %param.2, f32[8192]{0:T(1024)S(1)} %fusion.18, f32[512]{0:T(512)S(1)} %broadcast_divide_fusion.3), kind=kOutput, calls=%fused_computation.11 | convolution fusion | flops 25782386688 | bytes 9472000 | tf_op jit(solution)/shard_map/dot_general | solution.py:37
  182.2 0.0 reduce-scatter.3.cloned.1.call-update
  182.2 0.1 dynamic-slice_multiply_fusion.1
  182.3 50.7 %reduce-scatter.5.cloned.1.call-done = f32[16,512]{1,0:T(8,128)} async-done(((f32[512,512]{1,0:T(8,128)}), f32[16,512]{1,0:T(8,128)}) %reduce-scatter.5.cloned.1.call-update) | async-done | bytes 32784 | tf_op jit(solution)/shard_map/reduce_scatter | solution.py:53
  232.9 88.9 %reduce-scatter.3.cloned.1.call-done = f32[16,512]{1,0:T(8,128)} async-done(((f32[512,512]{1,0:T(8,128)}), f32[16,512]{1,0:T(8,128)}) %reduce-scatter.3.cloned.1.call-update) | async-done | bytes 32784 | tf_op jit(solution)/shard_map/reduce_scatter | solution.py:52
  321.8 1.4 multiply_add_fusion
  323.2 31.7 %all-reduce.3 = (f32[16,512]{1,0:T(8,128)S(1)}, f32[]{:T(128)}, f32[512]{0:T(512)S(1)}, f32[16,512]{1,0:T(8,128)S(1)}, f32[512]{0:T(512)S(1)}) all-reduce(f32[16,512]{1,0:T(8,128)S(1)} %get-tuple-element.20, f32[]{:T(128)S(6)} %convert_element_type.27, f32[512]{0:T(512)S(1)} %get-tuple-element.6, ...), channel_id=1, replica_groups=mesh['tm'=32,'group'=8] {'group'}, use_global_device_ids=true, to_apply=%region_6.0 | all-reduce | flops 17409 | bytes 139272 | tf_op jit(solution)/shard_map/psum | solution.py:60
  354.9 0.7 broadcast_divide_fusion
  355.6 0.8 dynamic-slice_multiply_fusion
  356.3 1.4 subtract_divide_fusion
  (3 shorter events, 0.0 us)
Async XLA Ops:
  7.2 225.8 %reduce-scatter.5.cloned.1.call-start = ((), (), s32[]{:S(2)}) async-start(), calls=%async_computation.3 | async-start | bytes 1081344 | tf_op jit(solution)/shard_map/reduce_scatter | solution.py:53
  10.3 28.5 %collective-permute-start = (bf16[2048,512]{1,0:T(8,128)(2,1)}, bf16[2048,512]{1,0:T(8,128)(2,1)S(1)}, u32[]{:S(2)}, u32[]{:S(2)}) collective-permute-start(bf16[2048,512]{1,0:T(8,128)(2,1)} %slice_bitcast_fusion.1), channel_id=1, source_target_pairs={{8,0},{16,8},{24,16},{32,24},{40,32},{48,40},{56,48},{64,56},{72,6... | collective-permute-start | bytes 6291464 | tf_op jit(solution)/shard_map/ppermute | solution.py:12
  15.6 23.2 %copy-start = (bf16[1,8192,512]{2,1,0:T(8,128)(2,1)S(1)}, bf16[1,8192,512]{2,1,0:T(8,128)(2,1)}, u32[]{:S(2)}) copy-start(bf16[1,8192,512]{2,1,0:T(8,128)(2,1)} %param.2) | copy-start | bytes 25165828
  19.0 31.1 %copy-start.1 = (bf16[6144,512]{1,0:T(8,128)(2,1)}, bf16[6144,512]{1,0:T(8,128)(2,1)S(1)}, u32[]{:S(2)}) copy-start(bf16[6144,512]{1,0:T(8,128)(2,1)S(1)} %slice_bitcast_fusion) | copy-start | bytes 18874372
  145.3 176.5 %reduce-scatter.3.cloned.1.call-start = ((), (), s32[]{:S(2)}) async-start(), calls=%async_computation.2 | async-start | bytes 1081344 | tf_op jit(solution)/shard_map/reduce_scatter | solution.py:52
Sparse Core Ops, SparseCore 0:
  145.5 87.4 reduce-scatter.4
  237.2 84.5 reduce-scatter.2
where the time goes:
time: 365 us
  waiting for transfers between devices  159 us (44%)
  blocking collectives  88.6 us (24%)
  matrix products  75 us (21%)
  other arithmetic  15.6 us (4%)
  between operations  14.8 us (4%)
  local copies, waits for them, and re-layouts  6.45 us (2%)
  starting transfers between devices  4.87 us (1%)
    reduce_scatter x1, waiting for transfers between devices, on_device(): lax.psum_scatter(inst, 'tm', scatter_dimension=0, tiled=True)  88.9 us
    psum x1, blocking collectives, on_device(): tot_x, tot_y = lax.psum((sum_x, sum_y), 'tm')  56.9 us
    reduce_scatter x1, waiting for transfers between devices, on_device(): lax.psum_scatter(lagm, 'tm', scatter_dimension=0, tiled=True)  50.7 us
    dot_general x1, matrix products, on_device(): lax.dot_general(cent_x, cent_y, contract, precision=lax.Precision.HIGHEST...  38.4 us
    dot_general x1, matrix products, on_device(): lax.dot_general(cent_x, cent_x, contract, precision=lax.Precision.HIGHEST...  36.6 us
    psum x1, blocking collectives, on_device(): lax.psum((part_inst, part_lag, tot_x, tot_y, number.reshape(1)), 'group')  31.7 us
    ppermute x1, waiting for transfers between devices, passed_along(): return lax.ppermute(block, axis, route)  19.8 us
    reduce_sum x1, other arithmetic, on_device(): sum_y = jnp.sum(later * weight, axis=0)  11.3 us
  transfers between devices with their start and end apart: 3, of which 3 were waited for; matrix products, arithmetic and copies ran while one was open for 11% of the time, Pallas kernels for 0%

commit v1 on v0

v1 whole, which is shorter than its diff:
```python
import functools

import jax
import jax.numpy as jnp
from jax import lax
from jax.experimental import pallas as pl
from jax.experimental.pallas import tpu as pltpu
from jax.sharding import PartitionSpec as P

LAG = 2048
BLK = 1024
LANES = 128
F32 = jnp.float32
CONTRACT = (((0,), (0,)), ((), ()))
VMEM_LIMIT = 48 * 1024 * 1024


def rows_below(limit, shape):
    return lax.broadcasted_iota(jnp.int32, shape, 0) < limit


def keep_below(block, limit):
    wide = jnp.where(rows_below(limit, block.shape), block.astype(F32), 0.0)
    return wide.astype(block.dtype)


def write_chunks(core, acc, tail, keep_ref, send_ref):
    chips, _, _ = keep_ref.shape
    width = acc.shape[1]
    share = acc.shape[0] // (2 * chips)
    for out, which in ((keep_ref, core), (send_ref, 1 - core)):
        for chip in range(chips):
            first = pl.multiple_of((2 * chip + which) * share, share)
            for col in range(width // LANES):
                out[chip, col * share : (col + 1) * share, :] = acc[
                    pl.ds(first, share), col * LANES : (col + 1) * LANES
                ]
            out[chip, share * (width // LANES) :, :] = tail


def tail_rows(sums, valid):
    width = sums.shape[1]
    parts = [sums[:, c * LANES : (c + 1) * LANES] for c in range(width // LANES)]
    count = jnp.full((8 - len(parts), LANES), valid, jnp.int32).astype(F32)
    return jnp.concatenate([*parts, count], axis=0)


def instant_kernel(
    place, x_hbm, keep_ref, send_ref, sum_y_ref, xs, acc, sum_x, sum_y, sems
):
    core, base, count = place[0], place[1], place[2]
    rows = xs.shape[0]
    blocks = rows // BLK

    def copy(b):
        part = pl.ds(b * BLK, BLK)
        return pltpu.make_async_copy(x_hbm.at[part], xs.at[part], sems.at[b])

    for b in range(blocks):
        copy(b).start()
    acc[...] = jnp.zeros_like(acc)
    sum_x[...] = jnp.zeros_like(sum_x)
    sum_y[...] = jnp.zeros_like(sum_y)

    def column_sum(wide):
        return jnp.sum(wide, axis=0, keepdims=True)

    for b in range(blocks):
        copy(b).wait()
        first = base + b * BLK
        full = first + BLK <= count

        @pl.when(full)
        def _():
            block = xs[b * BLK : (b + 1) * BLK, :]
            acc[...] += lax.dot_general(block, block, CONTRACT, preferred_element_type=F32)
            total = column_sum(block.astype(F32))
            sum_x[...] += total
            sum_y[...] += total * jnp.where(first >= LAG, 1.0, 0.0)

        @pl.when(jnp.logical_and(jnp.logical_not(full), first < count + LAG))
        def _():
            block = xs[b * BLK : (b + 1) * BLK, :]
            wide = block.astype(F32)
            held = jnp.where(rows_below(count - first, wide.shape), wide, 0.0)
            acc[...] += lax.dot_general(
                held.astype(block.dtype), block, CONTRACT, preferred_element_type=F32
            )
            later = jnp.where(rows_below(count + LAG - first, wide.shape), wide, 0.0)
            sum_x[...] += column_sum(held)
            sum_y[...] += column_sum(later) * jnp.where(first >= LAG, 1.0, 0.0)

    valid = jnp.clip(count - base, 0, rows)
    write_chunks(core, acc, tail_rows(sum_x[...], valid), keep_ref, send_ref)
    sum_y_ref[...] = jnp.broadcast_to(sum_y[...], sum_y_ref.shape)


def lagged_kernel(
    place, x_hbm, y_hbm, w_hbm, sum_y_ref, keep_ref, send_ref, xs, ys, ws, acc, sems
):
    core, base, count = place[0], place[1], place[2]
    rows = xs.shape[0]
    blocks = rows // BLK
    ahead = LAG // BLK

    def copy(b):
        part = pl.ds(b * BLK, BLK)
        return pltpu.make_async_copy(x_hbm.at[part], xs.at[part], sems.at[b])

    from_next = pltpu.make_async_copy(y_hbm, ys, sems.at[blocks])
    from_last = pltpu.make_async_copy(w_hbm, ws, sems.at[blocks + 1])
    for b in range(blocks):
        copy(b).start()
    from_next.start()
    from_last.start()
    acc[...] = jnp.zeros_like(acc)

    def add(first, early, late):
        full = first + BLK <= count

        @pl.when(full)
        def _():
            acc[...] += lax.dot_general(
                early[...], late[...], CONTRACT, preferred_element_type=F32
            )

        @pl.when(jnp.logical_and(jnp.logical_not(full), first < count))
        def _():
            acc[...] += lax.dot_general(
                keep_below(early[...], count - first),
                late[...],
                CONTRACT,
                preferred_element_type=F32,
            )

    def part(b):
        return xs.at[pl.ds(b * BLK, BLK)]

    for b in range(ahead):
        copy(b).wait()
    for b in range(blocks - ahead):
        copy(b + ahead).wait()
        add(base + b * BLK, part(b), part(b + ahead))
    from_next.wait()
    add(base + (blocks - ahead) * BLK, part(blocks - ahead), ys)
    from_last.wait()
    add(base - BLK, ws, part(1))
    valid = jnp.clip(count - base, 0, rows)
    write_chunks(core, acc, tail_rows(sum_y_ref[0:1, :], valid), keep_ref, send_ref)


def row_of(rows):
    return jnp.concatenate([rows[c : c + 1, :] for c in range(rows.shape[0])], axis=1)


def centered(total, mean_rows, mean_cols, number, share, out_ref):
    for col in range(out_ref.shape[1] // LANES):
        lanes = slice(col * LANES, (col + 1) * LANES)
        block = total[col * share : (col + 1) * share, :]
        out_ref[:, lanes] = block / number - mean_rows * mean_cols[:, lanes]


def finish(total_i, total_l, first_row, inst_ref, lag_ref):
    share, width = inst_ref.shape
    cols = width // LANES
    tail = share * cols
    number = total_i[tail + cols : tail + cols + 1, 0:1]
    mean_x = row_of(total_i[tail : tail + cols, :]) / number
    mean_y = row_of(total_l[tail : tail + cols, :]) / number
    row = lax.broadcasted_iota(jnp.int32, (share, width), 0)
    col = lax.broadcasted_iota(jnp.int32, (share, width), 1)
    own = jnp.where(col == row + first_row, jnp.broadcast_to(mean_x, (share, width)), 0.0)
    mean_rows = jnp.sum(own, axis=1, keepdims=True)
    centered(total_i, mean_rows, mean_x, number, share, inst_ref)
    centered(total_l, mean_rows, mean_y, number, share, lag_ref)


def session_kernel(place, parts_ref, inst_ref, lag_ref, total_ref):
    total = jnp.sum(parts_ref[...], axis=0)
    half = total.shape[0] // 2
    total_ref[...] = jnp.broadcast_to(total[None], total_ref.shape)
    finish(total[:half], total[half:], place[3], inst_ref, lag_ref)


def pooled_kernel(place, parts_ref, inst_ref, lag_ref):
    total = jnp.sum(parts_ref[...], axis=0)
    half = total.shape[0] // 2
    finish(total[:half], total[half:], place[3], inst_ref, lag_ref)


def on_device(frames, pair_count):
    local = frames[0]
    rows, width = local.shape
    blocks = rows // BLK
    parts = lax.axis_size("tm")
    sessions = lax.axis_size("group")
    chips = parts // 2
    share = width // parts
    chunk = share * (width // LANES) + 8
    me = lax.axis_index("tm")
    core = me % 2
    place = jnp.stack([core, me * rows, pair_count[0], me * share]).astype(jnp.int32)

    back = [(i, i - 1) for i in range(1, parts)]
    forth = [(i, i + 1) for i in range(parts - 1)]
    from_next = lax.ppermute(local[:BLK], "tm", back)
    from_last = lax.ppermute(local[rows - BLK :], "tm", forth)

    smem = pl.BlockSpec(memory_space=pltpu.SMEM)
    vmem = pl.BlockSpec(memory_space=pltpu.VMEM)
    hbm = pl.BlockSpec(memory_space=pl.ANY)
    half = jax.ShapeDtypeStruct((chips, chunk, LANES), F32)
    params = pltpu.CompilerParams(vmem_limit_bytes=VMEM_LIMIT)

    def cost(flops, moved):
        return pl.CostEstimate(flops=flops, bytes_accessed=moved, transcendentals=0)

    work = 2 * rows * width * width
    keep_i, send_i, sum_y = pl.pallas_call(
        instant_kernel,
        out_shape=(half, half, jax.ShapeDtypeStruct((8, width), F32)),
        in_specs=[smem, hbm],
        out_specs=(vmem, vmem, vmem),
        scratch_shapes=[
            pltpu.VMEM((rows, width), local.dtype),
            pltpu.VMEM((width, width), F32),
            pltpu.VMEM((1, width), F32),
            pltpu.VMEM((1, width), F32),
            pltpu.SemaphoreType.DMA((blocks,)),
        ],
        compiler_params=params,
        cost_estimate=cost(work, 10 << 20),
        name="instant",
    )(place, local)
    keep_l, send_l = pl.pallas_call(
        lagged_kernel,
        out_shape=(half, half),
        in_specs=[smem, hbm, hbm, hbm, vmem],
        out_specs=(vmem, vmem),
        scratch_shapes=[
            pltpu.VMEM((rows, width), local.dtype),
            pltpu.VMEM((BLK, width), local.dtype),
            pltpu.VMEM((BLK, width), local.dtype),
            pltpu.VMEM((width, width), F32),
            pltpu.SemaphoreType.DMA((blocks + 2,)),
        ],
        compiler_params=params,
        cost_estimate=cost(work, 12 << 20),
        name="lagged",
    )(place, local, from_next, from_last, sum_y)

    swap = [(i, i ^ 1) for i in range(parts)]
    both_i = keep_i + lax.ppermute(send_i, "tm", swap)
    both_l = keep_l + lax.ppermute(send_l, "tm", swap)
    both = jnp.concatenate([both_i, both_l], axis=1)
    same_core = [[2 * i + c for i in range(chips)] for c in range(2)]
    met = lax.all_to_all(both, "tm", 0, 0, axis_index_groups=same_core, tiled=True)

    out = jax.ShapeDtypeStruct((share, width), F32)
    group_instant, group_lagged, total = pl.pallas_call(
        session_kernel,
        out_shape=(out, out, jax.ShapeDtypeStruct((sessions, 2 * chunk, LANES), F32)),
        in_specs=[smem, vmem],
        out_specs=(vmem, vmem, vmem),
        compiler_params=params,
        name="session",
    )(place, met)
    all_total = lax.all_to_all(total, "group", 0, 0, tiled=True)
    pooled_instant, pooled_lagged = pl.pallas_call(
        pooled_kernel,
        out_shape=(out, out),
        in_specs=[smem, vmem],
        out_specs=(vmem, vmem),
        compiler_params=params,
        name="pooled",
    )(place, all_total)
    return (group_instant[None], group_lagged[None], pooled_instant, pooled_lagged)


def solution(mesh):
    in_specs = (P("group", "tm", None), P("group"))
    out_specs = (P("group", "tm", None), P("group", "tm", None), P("tm", None), P("tm", None))
    return jax.shard_map(
        on_device, mesh=mesh, in_specs=in_specs, out_specs=out_specs, check_vma=False
    )
```

time: 365 us -> 88.2 us (0.24)
  waiting for transfers between devices: 159 us -> 9.27 us
  matrix products: 75 us -> 0 us
  blocking collectives: 88.6 us -> 55.4 us
  other arithmetic: 15.6 us -> 0.28 us
  between operations: 14.8 us -> 1.37 us
  Pallas kernels: 0 us -> 10.9 us
  local copies, waits for them, and re-layouts: 6.45 us -> 2.65 us
    reduce_scatter x2 -> x0, waiting for transfers between devices: 140 us -> none  [the longest x1 88.9 us: on_device(): lax.psum_scatter(inst, 'tm', scatter_dimension=0, tiled=True)]
    psum x2 -> x0, blocking collectives: 88.6 us -> none  [the longest x1 56.9 us: on_device(): tot_x, tot_y = lax.psum((sum_x, sum_y), 'tm')]
    dot_general x2 -> x0, matrix products: 75 us -> none  [the longest x1 38.4 us: on_device(): lax.dot_general(cent_x, cent_y, contract, precision=lax.Precision.HIGHEST...]
    all_to_all x0 -> x2, blocking collectives: none -> 55.4 us  [the longest x1 27.8 us: on_device(): lax.all_to_all(both, 'tm', 0, 0, axis_index_groups=same_core, tiled=True)]
    reduce_sum x1 -> x0, other arithmetic: 11.3 us -> none  [on_device(): sum_y = jnp.sum(later * weight, axis=0)]
    pallas_call x0 -> x4, Pallas kernels: none -> 10.9 us  [the longest x1 4.11 us: on_device(): pl.pallas_call(lagged_kernel, out_shape=(half, half), in_specs=[smem, hbm...]
    ppermute x1 -> x4, waiting for transfers between devices: 19.8 us -> 9.27 us  [the longest x1 5.81 us: on_device(): from_last = lax.ppermute(local[rows - BLK:], 'tm', forth)]
    slice x2 -> x1, local copies, waits for them, and re-layouts: 6.44 us -> 2.65 us  [on_device(): from_last = lax.ppermute(local[rows - BLK:], 'tm', forth)]
  transfers between devices with their start and end apart: 3 -> 4, of which waited for: 3 -> 3; matrix products, arithmetic and copies ran while one was open for 11% -> 0% of each run, Pallas kernels for 0% -> 9%
where the time goes in v1:
time: 88.2 us; the launch traced here: 87.7 us
  blocking collectives  55.4 us (63%)
  Pallas kernels  10.9 us (12%)
  waiting for transfers between devices  9.27 us (11%)
  starting transfers between devices  7.84 us (9%)
  local copies, waits for them, and re-layouts  2.65 us (3%)
  between operations  1.37 us (2%)
    all_to_all x1, blocking collectives, on_device(): lax.all_to_all(both, 'tm', 0, 0, axis_index_groups=same_core, tiled=True)  27.8 us
    all_to_all x1, blocking collectives, on_device(): all_total = lax.all_to_all(total, 'group', 0, 0, tiled=True)  27.6 us
    ppermute x1, waiting for transfers between devices, on_device(): from_last = lax.ppermute(local[rows - BLK:], 'tm', forth)  5.81 us
    ppermute x1, starting transfers between devices, on_device(): from_next = lax.ppermute(local[:BLK], 'tm', back)  5.75 us
    pallas_call x1, Pallas kernels, on_device(): pl.pallas_call(lagged_kernel, out_shape=(half, half), in_specs=[smem, hbm...  4.11 us
    pallas_call x1, Pallas kernels, on_device(): pl.pallas_call(instant_kernel, out_shape=(half, half, jax.ShapeDtypeStruc...  4.1 us
    slice x1, local copies, waits for them, and re-layouts, on_device(): from_last = lax.ppermute(local[rows - BLK:], 'tm', forth)  2.65 us
    ppermute x1, waiting for transfers between devices, on_device(): both_l = keep_l + lax.ppermute(send_l, 'tm', swap)  1.91 us
  transfers between devices with their start and end apart: 4, of which 3 were waited for; matrix products, arithmetic and copies ran while one was open for 0% of the time, Pallas kernels for 9%

profile of v1, /device:TPU:6, one launch (start us, length us, event | category | flops | bytes accessed | tf_op | source)
XLA Modules:
  0.0 87.7 jit_solution(10381610976002661485)
XLA Ops:
  0.6 2.6 %slice_bitcast_fusion = (bf16[1024,512]{1,0:T(8,128)(2,1)}, bf16[1024,512]{1,0:T(8,128)(2,1)S(1)}) fusion(bf16[1,8192,512]{2,1,0:T(8,128)(2,1)} %param.2), kind=kLoop, calls=%fused_computation.1 | loop fusion | bytes 4194304 | tf_op jit(solution)/shard_map/slice | solution.py:207
  3.3 1.9 %collective-permute-start.2 = (bf16[1024,512]{1,0:T(8,128)(2,1)}, bf16[1024,512]{1,0:T(8,128)(2,1)S(1)}, u32[]{:S(2)}, u32[]{:S(2)}) collective-permute-start(bf16[1024,512]{1,0:T(8,128)(2,1)} %get-tuple-element.24), channel_id=1, source_target_pairs={{0,8},{8,16},{16,24},{24,32},{32,40},{40,48},{48,56},{56,64},{64,7... | collective-permute-start | bytes 3145736 | tf_op jit(solution)/shard_map/ppermute | solution.py:207
  5.2 5.8 %collective-permute-start.1 = (bf16[1024,512]{1,0:T(8,128)(2,1)S(1)}, bf16[1024,512]{1,0:T(8,128)(2,1)S(1)}, u32[]{:S(2)}, u32[]{:S(2)}) collective-permute-start(bf16[1024,512]{1,0:T(8,128)(2,1)S(1)} %get-tuple-element.25), channel_id=1, source_target_pairs={{8,0},{16,8},{24,16},{32,24},{40,32},{48,40},{56,48},{64,56},{72,6... | collective-permute-start | bytes 3145736 | tf_op jit(solution)/shard_map/ppermute | solution.py:206
  11.6 0.1 pad_add_fusion.place
  11.7 4.1 %instant.1 = (f32[16,72,128]{2,1,0:T(8,128)S(1)}, f32[16,72,128]{2,1,0:T(8,128)S(1)}, f32[8,512]{1,0:T(8,128)S(1)}) custom-call(s32[4]{0:T(128)S(1)} %pad_add_fusion.place, bf16[8192,512]{1,0:T(8,128)(2,1)} %bitcast.10), custom_call_target="tpu_custom_call" | custom-call | flops 4294967296 | bytes 10485760 | tf_op jit(solution)/shard_map/instant/pallas_call | solution.py:219
  15.8 0.1 collective-permute-start
  15.9 5.8 %collective-permute-done.2.w_hbm = bf16[1024,512]{1,0:T(8,128)(2,1)S(1)} collective-permute-done((bf16[1024,512]{1,0:T(8,128)(2,1)}, bf16[1024,512]{1,0:T(8,128)(2,1)S(1)}, u32[]{:S(2)}, u32[]{:S(2)}) %collective-permute-start.2) | collective-permute-done | bytes 1048608 | tf_op jit(solution)/shard_map/ppermute | solution.py:207
  21.7 1.5 %collective-permute-done.1.y_hbm = bf16[1024,512]{1,0:T(8,128)(2,1)S(1)} collective-permute-done((bf16[1024,512]{1,0:T(8,128)(2,1)S(1)}, bf16[1024,512]{1,0:T(8,128)(2,1)S(1)}, u32[]{:S(2)}, u32[]{:S(2)}) %collective-permute-start.1) | collective-permute-done | bytes 1048608 | tf_op jit(solution)/shard_map/ppermute | solution.py:206
  23.2 4.1 %lagged.1 = (f32[16,72,128]{2,1,0:T(8,128)S(1)}, f32[16,72,128]{2,1,0:T(8,128)S(1)}) custom-call(s32[4]{0:T(128)S(1)} %pad_add_fusion.place, bf16[8192,512]{1,0:T(8,128)(2,1)} %bitcast.11, bf16[1024,512]{1,0:T(8,128)(2,1)S(1)} %collective-permute-done.1.y_hbm, bf16[1024,512]{1,0:T(8,128)(2,1)S(1)} %collective-permute-done.2.w_hbm, ...), custom_call_target="tpu_custom_call" | custom-call | flops 4294967296 | bytes 12582912 | tf_op jit(solution)/shard_map/lagged/pallas_call | solution.py:235
  27.4 0.1 collective-permute-start.3
  27.5 0.0 collective-permute-done
  27.5 0.1 add.11
  27.6 1.9 %collective-permute-done.3 = f32[16,72,128]{2,1,0:T(8,128)S(1)} collective-permute-done((f32[16,72,128]{2,1,0:T(8,128)S(1)}, f32[16,72,128]{2,1,0:T(8,128)S(1)}, u32[]{:S(2)}, u32[]{:S(2)}) %collective-permute-start.3) | collective-permute-done | bytes 589856 | tf_op jit(solution)/shard_map/ppermute | solution.py:254
  29.5 0.1 add.12
  29.5 0.1 pad_maximum_fusion
  29.6 27.8 %all_to_all.10.parts_ref = f32[16,144,128]{2,1,0:T(8,128)S(1)} all-to-all(f32[16,144,128]{2,1,0:T(8,128)S(1)} %pad_maximum_fusion), channel_id=1, replica_groups={{0,16,32,48,64,80,96,112,128,144,160,176,192,208,224,240},{8,24,40,56,7..., dimensions={0} | all-to-all | bytes 2359296 | tf_op jit(solution)/shard_map/all_to_all | solution.py:257
  57.4 1.3 %session.1 = (f32[16,512]{1,0:T(8,128)}, f32[16,512]{1,0:T(8,128)}, f32[8,144,128]{2,1,0:T(8,128)S(1)}) custom-call(s32[4]{0:T(128)S(1)} %pad_add_fusion.place, f32[16,144,128]{2,1,0:T(8,128)S(1)} %all_to_all.10.parts_ref), custom_call_target="tpu_custom_call" | custom-call | tf_op jit(solution)/shard_map/session/pallas_call | solution.py:260
  58.8 27.6 %all_to_all.11.parts_ref = f32[8,144,128]{2,1,0:T(8,128)S(1)} all-to-all(f32[8,144,128]{2,1,0:T(8,128)S(1)} %get-tuple-element.21), channel_id=1, replica_groups=mesh['tm'=32,'group'=8] {'group'}, dimensions={0} | all-to-all | bytes 1179648 | tf_op jit(solution)/shard_map/all_to_all | solution.py:268
  86.4 1.3 %pooled.1 = (f32[16,512]{1,0:T(8,128)}, f32[16,512]{1,0:T(8,128)}) custom-call(s32[4]{0:T(128)S(1)} %pad_add_fusion.place, f32[8,144,128]{2,1,0:T(8,128)S(1)} %all_to_all.11.parts_ref), custom_call_target="tpu_custom_call" | custom-call | tf_op jit(solution)/shard_map/pooled/pallas_call | solution.py:269
Async XLA Ops:
  3.3 18.4 %collective-permute-start.2 = (bf16[1024,512]{1,0:T(8,128)(2,1)}, bf16[1024,512]{1,0:T(8,128)(2,1)S(1)}, u32[]{:S(2)}, u32[]{:S(2)}) collective-permute-start(bf16[1024,512]{1,0:T(8,128)(2,1)} %get-tuple-element.24), channel_id=1, source_target_pairs={{0,8},{8,16},{16,24},{24,32},{32,40},{40,48},{48,56},{56,64},{64,7... | collective-permute-start | bytes 3145736 | tf_op jit(solution)/shard_map/ppermute | solution.py:207
  5.2 18.1 %collective-permute-start.1 = (bf16[1024,512]{1,0:T(8,128)(2,1)S(1)}, bf16[1024,512]{1,0:T(8,128)(2,1)S(1)}, u32[]{:S(2)}, u32[]{:S(2)}) collective-permute-start(bf16[1024,512]{1,0:T(8,128)(2,1)S(1)} %get-tuple-element.25), channel_id=1, source_target_pairs={{8,0},{16,8},{24,16},{32,24},{40,32},{48,40},{56,48},{64,56},{72,6... | collective-permute-start | bytes 3145736 | tf_op jit(solution)/shard_map/ppermute | solution.py:206
  15.8 11.7 %collective-permute-start = (f32[16,72,128]{2,1,0:T(8,128)S(1)}, f32[16,72,128]{2,1,0:T(8,128)S(1)}, u32[]{:S(2)}, u32[]{:S(2)}) collective-permute-start(f32[16,72,128]{2,1,0:T(8,128)S(1)} %get-tuple-element.15), channel_id=1, source_target_pairs={{0,8},{8,0},{16,24},{24,16},{32,40},{40,32},{48,56},{56,48},{64,72... | collective-permute-start | bytes 1769480 | tf_op jit(solution)/shard_map/ppermute | solution.py:253
  27.4 2.1 %collective-permute-start.3 = (f32[16,72,128]{2,1,0:T(8,128)S(1)}, f32[16,72,128]{2,1,0:T(8,128)S(1)}, u32[]{:S(2)}, u32[]{:S(2)}) collective-permute-start(f32[16,72,128]{2,1,0:T(8,128)S(1)} %get-tuple-element.18), channel_id=1, source_target_pairs={{0,8},{8,0},{16,24},{24,16},{32,40},{40,32},{48,56},{56,48},{64,72... | collective-permute-start | bytes 1769480 | tf_op jit(solution)/shard_map/ppermute | solution.py:254

commit v2 on v0

v2 whole, which is shorter than its diff:
```python
import math

import jax
import jax.numpy as jnp
from jax import lax
from jax.experimental import pallas as pl
from jax.experimental.pallas import tpu as pltpu
from jax.sharding import PartitionSpec as P

LAG = 2048
BLK = 1024
LANES = 128
F32 = jnp.float32
CONTRACT = (((0,), (0,)), ((), ()))
VMEM_LIMIT = 48 * 1024 * 1024


def rows_below(limit, shape):
    return lax.broadcasted_iota(jnp.int32, shape, 0) < limit


def keep_below(block, limit):
    wide = jnp.where(rows_below(limit, block.shape), block.astype(F32), 0.0)
    return wide.astype(block.dtype)


def write_chunks(place, acc, tail, keep_ref, send_ref, x_first):
    core, my_x, my_y = place[0], place[4], place[5]
    side = keep_ref.shape[0]
    width = acc.shape[1]
    share = acc.shape[0] // (2 * side * side)
    for out, which in ((keep_ref, core), (send_ref, 1 - core)):
        for i in range(side):
            for j in range(side):
                far_x, far_y = (i, j) if x_first else (j, i)
                chip = lax.rem(my_x + far_x, side) * side + lax.rem(my_y + far_y, side)
                first = pl.multiple_of((2 * chip + which) * share, share)
                for col in range(width // LANES):
                    out[i, j, col * share : (col + 1) * share, :] = acc[
                        pl.ds(first, share), col * LANES : (col + 1) * LANES
                    ]
                out[i, j, share * (width // LANES) :, :] = tail


def tail_rows(sums, valid):
    width = sums.shape[1]
    parts = [sums[:, c * LANES : (c + 1) * LANES] for c in range(width // LANES)]
    count = jnp.full((8 - len(parts), LANES), valid, jnp.int32).astype(F32)
    return jnp.concatenate([*parts, count], axis=0)


def moments_kernel(
    place, x_hbm, keep_ref, send_ref, lag, sum_y_ref, xs, acc, sum_x, sum_y, sems
):
    base, count = place[1], place[2]
    rows = xs.shape[0]
    blocks = rows // BLK
    ahead = LAG // BLK

    def copy(b):
        part = pl.ds(b * BLK, BLK)
        return pltpu.make_async_copy(x_hbm.at[part], xs.at[part], sems.at[b])

    for b in range(blocks):
        copy(b).start()
    acc[...] = jnp.zeros_like(acc)
    lag[...] = jnp.zeros_like(lag)
    sum_x[...] = jnp.zeros_like(sum_x)
    sum_y[...] = jnp.zeros_like(sum_y)

    def column_sum(wide):
        return jnp.sum(wide, axis=0, keepdims=True)

    def multiply(b, early):
        turned = early.T
        acc[...] += jnp.dot(turned, xs[b * BLK : (b + 1) * BLK, :], preferred_element_type=F32)
        if b + ahead < blocks:
            late = xs[(b + ahead) * BLK : (b + ahead + 1) * BLK, :]
            lag[...] += jnp.dot(turned, late, preferred_element_type=F32)

    for b in range(ahead):
        copy(b).wait()
    for b in range(blocks):
        if b + ahead < blocks:
            copy(b + ahead).wait()
        first = base + b * BLK
        full = first + BLK <= count

        @pl.when(full)
        def _():
            block = xs[b * BLK : (b + 1) * BLK, :]
            multiply(b, block)
            total = column_sum(block.astype(F32))
            sum_x[...] += total
            sum_y[...] += total * jnp.where(first >= LAG, 1.0, 0.0)

        @pl.when(jnp.logical_and(jnp.logical_not(full), first < count + LAG))
        def _():
            wide = xs[b * BLK : (b + 1) * BLK, :].astype(F32)
            held = jnp.where(rows_below(count - first, wide.shape), wide, 0.0)
            multiply(b, held.astype(xs.dtype))
            later = jnp.where(rows_below(count + LAG - first, wide.shape), wide, 0.0)
            sum_x[...] += column_sum(held)
            sum_y[...] += column_sum(later) * jnp.where(first >= LAG, 1.0, 0.0)

    valid = jnp.clip(count - base, 0, rows)
    write_chunks(place, acc, tail_rows(sum_x[...], valid), keep_ref, send_ref, False)
    sum_y_ref[...] = jnp.broadcast_to(sum_y[...], sum_y_ref.shape)


def border_kernel(
    place, x_hbm, y_ref, w_ref, part_ref, sum_y_ref, keep_ref, send_ref, xs, acc, sems
):
    base, count = place[1], place[2]
    rows = x_hbm.shape[0]
    last = rows - LAG

    def copy(k, first):
        return pltpu.make_async_copy(x_hbm.at[pl.ds(first, BLK)], xs.at[k], sems.at[k])

    copies = [copy(0, last), copy(1, BLK)]
    for each in copies:
        each.start()
    for each in copies:
        each.wait()
    full = base + last + BLK <= count

    @pl.when(full)
    def _():
        acc[...] = (
            part_ref[...]
            + lax.dot_general(xs[0], y_ref[...], CONTRACT, preferred_element_type=F32)
            + lax.dot_general(w_ref[...], xs[1], CONTRACT, preferred_element_type=F32)
        )

    @pl.when(jnp.logical_not(full))
    def _():
        early = keep_below(xs[0], count - base - last)
        before = keep_below(w_ref[...], count - base + BLK)
        acc[...] = (
            part_ref[...]
            + lax.dot_general(early, y_ref[...], CONTRACT, preferred_element_type=F32)
            + lax.dot_general(before, xs[1], CONTRACT, preferred_element_type=F32)
        )

    valid = jnp.clip(count - base, 0, rows)
    write_chunks(place, acc, tail_rows(sum_y_ref[0:1, :], valid), keep_ref, send_ref, True)


def edges_kernel(x_hbm, top_ref, end_ref, sems):
    rows, height = x_hbm.shape[0], top_ref.shape[0]
    top = pltpu.make_async_copy(x_hbm.at[pl.ds(0, height)], top_ref, sems.at[0])
    end = pltpu.make_async_copy(x_hbm.at[pl.ds(rows - height, height)], end_ref, sems.at[1])
    top.start()
    end.start()
    top.wait()
    end.wait()


def pair_kernel(keep_ref, met_ref, *outs):
    for d, out in enumerate(outs):
        out[...] = keep_ref[d] + met_ref[d]


def line_kernel(*refs):
    side = len(refs) // 2
    ins, outs = refs[:side], refs[side:]
    for d, out in enumerate(outs):
        out[...] = (ins[0][d] + ins[1][d]) + (ins[2][d] + ins[3][d])


def row_of(rows):
    return jnp.concatenate([rows[c : c + 1, :] for c in range(rows.shape[0])], axis=1)


def centered(total, mean_rows, mean_cols, number, share, out_ref):
    for col in range(out_ref.shape[1] // LANES):
        lanes = slice(col * LANES, (col + 1) * LANES)
        block = total[col * share : (col + 1) * share, :]
        out_ref[:, lanes] = block / number - mean_rows * mean_cols[:, lanes]


def finish(total_i, total_l, first_row, inst_ref, lag_ref):
    share, width = inst_ref.shape
    cols = width // LANES
    tail = share * cols
    number = total_i[tail + cols : tail + cols + 1, 0:1]
    mean_x = row_of(total_i[tail : tail + cols, :]) / number
    mean_y = row_of(total_l[tail : tail + cols, :]) / number
    row = lax.broadcasted_iota(jnp.int32, (share, width), 0)
    col = lax.broadcasted_iota(jnp.int32, (share, width), 1)
    own = jnp.where(col == row + first_row, jnp.broadcast_to(mean_x, (share, width)), 0.0)
    mean_rows = jnp.sum(own, axis=1, keepdims=True)
    centered(total_i, mean_rows, mean_x, number, share, inst_ref)
    centered(total_l, mean_rows, mean_y, number, share, lag_ref)


def session_kernel(place, *refs):
    inst_ref, lag_ref, total_ref = refs[-3:]
    parts = refs[:-3]
    half = total_ref.shape[0] // 2
    side = len(parts) // 2
    for k in range(2):
        a, b, c, d = parts[k * side : (k + 1) * side]
        total_ref[k * half : (k + 1) * half, :] = (a[...] + b[...]) + (c[...] + d[...])
    finish(total_ref[:half], total_ref[half:], place[3], inst_ref, lag_ref)


def duo_kernel(a_ref, b_ref, out_ref):
    out_ref[...] = a_ref[...] + b_ref[...]


def pooled_kernel(place, a_ref, b_ref, inst_ref, lag_ref):
    total = a_ref[...] + b_ref[...]
    half = total.shape[0] // 2
    finish(total[:half], total[half:], place[3], inst_ref, lag_ref)


def on_device(frames, pair_count):
    local = frames[0]
    rows, width = local.shape
    blocks = rows // BLK
    parts = lax.axis_size("tm")
    sessions = lax.axis_size("group")
    side = math.isqrt(parts // 2)
    share = width // parts
    chunk = share * (width // LANES) + 8
    me = lax.axis_index("tm")
    numbers = [me % 2, me * rows, pair_count[0], me * share, me // (2 * side), (me // 2) % side]
    place = jnp.stack(numbers).astype(jnp.int32)

    smem = pl.BlockSpec(memory_space=pltpu.SMEM)
    vmem = pl.BlockSpec(memory_space=pltpu.VMEM)
    hbm = pl.BlockSpec(memory_space=pl.ANY)
    params = pltpu.CompilerParams(vmem_limit_bytes=VMEM_LIMIT)

    def floats(*shape):
        return jax.ShapeDtypeStruct(shape, F32)

    def call(kernel, name, ins, out_shape, scratch=(), flops=0, moved=0):
        specs = jax.tree.map(lambda _: vmem, out_shape)
        return pl.pallas_call(
            kernel,
            out_shape=out_shape,
            in_specs=[spec for _, spec in ins],
            out_specs=specs,
            scratch_shapes=list(scratch),
            compiler_params=params,
            cost_estimate=pl.CostEstimate(flops=flops, bytes_accessed=moved, transcendentals=0),
            name=name,
        )(*[operand for operand, _ in ins])

    def dma(n):
        return pltpu.SemaphoreType.DMA((n,))

    where, frames_in = (place, smem), (local, hbm)
    edge = jax.ShapeDtypeStruct((BLK, width), local.dtype)
    top, end = pl.pallas_call(
        edges_kernel,
        out_shape=(edge, edge),
        in_specs=[hbm],
        out_specs=(vmem, vmem),
        scratch_shapes=[dma(2)],
        compiler_params=params,
        name="edges",
    )(local)
    back = [(i, i - 1) for i in range(1, parts)]
    forth = [(i, i + 1) for i in range(parts - 1)]
    from_next = lax.ppermute(top, "tm", back)
    from_last = lax.ppermute(end, "tm", forth)

    swap = [(i, i ^ 1) for i in range(parts)]

    def at(x, y, c):
        return ((x % side) * side + y % side) * 2 + c

    def along(block, far_x, far_y):
        grid = [(x, y, c) for x in range(side) for y in range(side) for c in range(2)]
        route = [(at(x, y, c), at(x + far_x, y + far_y, c)) for x, y, c in grid]
        return lax.ppermute(block, "tm", route)

    def gather(blocks, on_x):
        moved = [along(blocks[d], d * on_x, d * (1 - on_x)) for d in range(1, side)]
        return [blocks[0], *moved]

    def over_plane(keep, send, x_first, name):
        met = lax.ppermute(send, "tm", swap)
        lines = call(pair_kernel, "pair_" + name, [(keep, vmem), (met, vmem)], [floats(side, chunk, LANES)] * side)
        came = gather(lines, x_first)
        cells = call(line_kernel, "line_" + name, [(v, vmem) for v in came], [floats(chunk, LANES)] * side)
        return gather(cells, 1 - x_first)

    half = floats(side, side, chunk, LANES)
    square = pltpu.VMEM((width, width), F32)
    held = pltpu.VMEM((rows, width), local.dtype)
    line = pltpu.VMEM((1, width), F32)
    work = 2 * rows * width * width
    keep_i, send_i, partial, sum_y = call(
        moments_kernel,
        "moments",
        [where, frames_in],
        (half, half, floats(width, width), floats(8, width)),
        [held, square, line, line, dma(blocks)],
        work * 7 // 4,
        rows * width * 2,
    )
    keep_l, send_l = call(
        border_kernel,
        "border",
        [where, frames_in, (from_next, vmem), (from_last, vmem), (partial, vmem), (sum_y, vmem)],
        (half, half),
        [pltpu.VMEM((2, BLK, width), local.dtype), square, dma(2)],
        work // 4,
        rows * width,
    )
    cells_i = over_plane(keep_i, send_i, 0, "instant")
    cells_l = over_plane(keep_l, send_l, 1, "lagged")
    out = floats(share, width)
    group_instant, group_lagged, total = call(
        session_kernel,
        "session",
        [where, *[(v, vmem) for v in (*cells_i, *cells_l)]],
        (out, out, floats(2 * chunk, LANES)),
    )
    for route in (lambda i: i ^ 1, lambda i: i ^ 2, lambda i: (sessions - 2 - (i & -2)) | (i & 1)):
        other = lax.ppermute(total, "group", [(i, route(i)) for i in range(sessions)])
        last = (total, other)
        total = call(duo_kernel, "duo", [(v, vmem) for v in last], floats(2 * chunk, LANES))
    pooled_instant, pooled_lagged = call(
        pooled_kernel, "pooled", [where, *[(v, vmem) for v in last]], (out, out)
    )
    return (group_instant[None], group_lagged[None], pooled_instant, pooled_lagged)


def solution(mesh):
    in_specs = (P("group", "tm", None), P("group"))
    out_specs = (P("group", "tm", None), P("group", "tm", None), P("tm", None), P("tm", None))
    return jax.shard_map(
        on_device, mesh=mesh, in_specs=in_specs, out_specs=out_specs, check_vma=False
    )
```

time: 365 us -> 76.1 us (0.21)
  waiting for transfers between devices: 159 us -> 20.7 us
  blocking collectives: 88.6 us -> 0 us
  matrix products: 75 us -> 0 us
  starting transfers between devices: 4.87 us -> 32.6 us
  Pallas kernels: 0 us -> 20.9 us
  other arithmetic: 15.6 us -> 0 us
  between operations: 14.8 us -> 1.46 us
  local copies, waits for them, and re-layouts: 6.45 us -> 0.08 us
    reduce_scatter x2 -> x0, waiting for transfers between devices: 140 us -> none  [the longest x1 88.9 us: on_device(): lax.psum_scatter(inst, 'tm', scatter_dimension=0, tiled=True)]
    psum x2 -> x0, blocking collectives: 88.6 us -> none  [the longest x1 56.9 us: on_device(): tot_x, tot_y = lax.psum((sum_x, sum_y), 'tm')]
    dot_general x2 -> x0, matrix products: 75 us -> none  [the longest x1 38.4 us: on_device(): lax.dot_general(cent_x, cent_y, contract, precision=lax.Precision.HIGHEST...]
    ppermute x1 -> x19, starting transfers between devices: 4.61 us -> 32.6 us  [the longest x12 13.7 us: along(): return lax.ppermute(block, 'tm', route)]
    pallas_call x0 -> x11, Pallas kernels: none -> 20.9 us  [the longest x10 18.3 us: call(): pl.pallas_call(kernel, out_shape=out_shape, in_specs=[spec for _, spec in...]
    reduce_sum x1 -> x0, other arithmetic: 11.3 us -> none  [on_device(): sum_y = jnp.sum(later * weight, axis=0)]
    slice x2 -> x0, local copies, waits for them, and re-layouts: 6.44 us -> none  [the longest x1 3.37 us: on_device(): lagged = jnp.concatenate([local[LAG:], incoming], axis=0)]
    ppermute x1 -> x19, waiting for transfers between devices: 19.8 us -> 20.7 us  [the longest x12 10.1 us: along(): return lax.ppermute(block, 'tm', route)]
  transfers between devices with their start and end apart: 3 -> 19, of which waited for: 3 -> 10; matrix products, arithmetic and copies ran while one was open for 11% -> 0% of each run, Pallas kernels for 0% -> 21%
where the time goes in v2:
time: 76.1 us; the launch traced here: 75.7 us
  starting transfers between devices  32.6 us (43%)
  Pallas kernels  20.9 us (27%)
  waiting for transfers between devices  20.7 us (27%)
  between operations  1.46 us (2%)
    pallas_call x10, Pallas kernels, call(): pl.pallas_call(kernel, out_shape=out_shape, in_specs=[spec for _, spec in...  18.3 us
    ppermute x12, starting transfers between devices, along(): return lax.ppermute(block, 'tm', route)  13.7 us
    ppermute x3, starting transfers between devices, on_device(): lax.ppermute(total, 'group', [(i, route(i)) for i in range(sessions)])  12.1 us
    ppermute x12, waiting for transfers between devices, along(): return lax.ppermute(block, 'tm', route)  10.1 us
    ppermute x3, waiting for transfers between devices, on_device(): lax.ppermute(total, 'group', [(i, route(i)) for i in range(sessions)])  7.17 us
    ppermute x1, starting transfers between devices, on_device(): from_next = lax.ppermute(top, 'tm', back)  4.63 us
    ppermute x1, waiting for transfers between devices, on_device(): from_last = lax.ppermute(end, 'tm', forth)  3.43 us
    pallas_call x1, Pallas kernels, on_device(): pl.pallas_call(edges_kernel, out_shape=(edge, edge), in_specs=[hbm], out_...  2.57 us
  transfers between devices with their start and end apart: 19, of which 10 were waited for; matrix products, arithmetic and copies ran while one was open for 0% of the time, Pallas kernels for 21%

profile of v2, /device:TPU:6, one launch (start us, length us, event | category | flops | bytes accessed | tf_op | source)
XLA Modules:
  0.0 75.7 jit_solution(5492645403141032184)
XLA Ops:
  0.6 2.6 %edges.1 = (bf16[1024,512]{1,0:T(8,128)(2,1)}, bf16[1024,512]{1,0:T(8,128)(2,1)S(1)}) custom-call(bf16[8192,512]{1,0:T(8,128)(2,1)} %bitcast.8), custom_call_target="tpu_custom_call" | custom-call | tf_op jit(solution)/shard_map/edges/pallas_call | solution.py:258
  3.2 4.6 %collective-permute-start.7 = (bf16[1024,512]{1,0:T(8,128)(2,1)}, bf16[1024,512]{1,0:T(8,128)(2,1)S(1)}, u32[]{:S(2)}, u32[]{:S(2)}) collective-permute-start(bf16[1024,512]{1,0:T(8,128)(2,1)} %get-tuple-element.43), channel_id=1, source_target_pairs={{8,0},{16,8},{24,16},{32,24},{40,32},{48,40},{56,48},{64,56},{72,6... | collective-permute-start | bytes 3145736 | tf_op jit(solution)/shard_map/ppermute | solution.py:269
  7.8 1.9 %collective-permute-start.8 = (bf16[1024,512]{1,0:T(8,128)(2,1)S(1)}, bf16[1024,512]{1,0:T(8,128)(2,1)S(1)}, u32[]{:S(2)}, u32[]{:S(2)}) collective-permute-start(bf16[1024,512]{1,0:T(8,128)(2,1)S(1)} %get-tuple-element.44), channel_id=1, source_target_pairs={{0,8},{8,16},{16,24},{24,32},{32,40},{40,48},{48,56},{56,64},{64,7... | collective-permute-start | bytes 3145736 | tf_op jit(solution)/shard_map/ppermute | solution.py:270
  10.5 12.0 %moments.1 = (f32[4,4,72,128]{3,2,1,0:T(8,128)S(1)}, f32[4,4,72,128]{3,2,1,0:T(8,128)S(1)}, f32[512,512]{1,0:T(8,128)S(1)}, f32[8,512]{1,0:T(8,128)S(1)}) custom-call(s32[6]{0:T(128)S(1)} %stack.23.place, bf16[8192,512]{1,0:T(8,128)(2,1)} %bitcast.9), custom_call_target="tpu_custom_call" | custom-call | flops 7516192768 | bytes 8388608 | tf_op jit(solution)/shard_map/moments/pallas_call | solution.py:242
  22.6 3.4 %collective-permute-done.8.w_ref = bf16[1024,512]{1,0:T(8,128)(2,1)S(1)} collective-permute-done((bf16[1024,512]{1,0:T(8,128)(2,1)S(1)}, bf16[1024,512]{1,0:T(8,128)(2,1)S(1)}, u32[]{:S(2)}, u32[]{:S(2)}) %collective-permute-start.8) | collective-permute-done | bytes 1048608 | tf_op jit(solution)/shard_map/ppermute | solution.py:270
  26.1 3.5 %border.1 = (f32[4,4,72,128]{3,2,1,0:T(8,128)S(1)}, f32[4,4,72,128]{3,2,1,0:T(8,128)S(1)}) custom-call(s32[6]{0:T(128)S(1)} %stack.23.place, bf16[8192,512]{1,0:T(8,128)(2,1)} %bitcast.10, bf16[1024,512]{1,0:T(8,128)(2,1)S(1)} %collective-permute-done.7.y_ref, bf16[1024,512]{1,0:T(8,128)(2,1)S(1)} %collective-permute-done.8.w_ref, ...), custom_call_target="tpu_custom_call" | custom-call | flops 1073741824 | bytes 4194304 | tf_op jit(solution)/shard_map/border/pallas_call | solution.py:242
  29.9 3.1 %collective-permute-start.3 = (f32[4,72,128]{2,1,0:T(8,128)S(1)}, f32[4,72,128]{2,1,0:T(8,128)S(1)}, u32[]{:S(2)}, u32[]{:S(2)}) collective-permute-start(f32[4,72,128]{2,1,0:T(8,128)S(1)} %get-tuple-element.38), channel_id=1, source_target_pairs={{0,48},{8,56},{16,0},{24,8},{32,16},{40,24},{48,32},{56,40},{64,11... | collective-permute-start | bytes 442376 | tf_op jit(solution)/shard_map/ppermute | solution.py:280
  33.2 2.6 %collective-permute-start.11 = (f32[4,72,128]{2,1,0:T(8,128)S(1)}, f32[4,72,128]{2,1,0:T(8,128)S(1)}, u32[]{:S(2)}, u32[]{:S(2)}) collective-permute-start(f32[4,72,128]{2,1,0:T(8,128)S(1)} %get-tuple-element.51), channel_id=1, source_target_pairs={{0,128},{8,136},{16,144},{24,152},{32,160},{40,168},{48,176},{56,1... | collective-permute-start | bytes 442376 | tf_op jit(solution)/shard_map/ppermute | solution.py:280
  35.8 4.6 %collective-permute-done.1.refs_1_ = f32[4,72,128]{2,1,0:T(8,128)S(1)} collective-permute-done((f32[4,72,128]{2,1,0:T(8,128)S(1)}, f32[4,72,128]{2,1,0:T(8,128)S(1)}, u32[]{:S(2)}, u32[]{:S(2)}) %collective-permute-start.1) | collective-permute-done | bytes 147488 | tf_op jit(solution)/shard_map/ppermute | solution.py:280
  41.1 2.9 %collective-permute-start.4 = (f32[72,128]{1,0:T(8,128)S(1)}, f32[72,128]{1,0:T(8,128)S(1)}, u32[]{:S(2)}, u32[]{:S(2)}) collective-permute-start(f32[72,128]{1,0:T(8,128)S(1)} %get-tuple-element.40), channel_id=1, source_target_pairs={{0,64},{8,72},{16,80},{24,88},{32,96},{40,104},{48,112},{56,120},{... | collective-permute-start | bytes 110600 | tf_op jit(solution)/shard_map/ppermute | solution.py:280
  44.0 1.0 %collective-permute-start.6 = (f32[72,128]{1,0:T(8,128)S(1)}, f32[72,128]{1,0:T(8,128)S(1)}, u32[]{:S(2)}, u32[]{:S(2)}) collective-permute-start(f32[72,128]{1,0:T(8,128)S(1)} %get-tuple-element.42), channel_id=1, source_target_pairs={{0,192},{8,200},{16,208},{24,216},{32,224},{40,232},{48,240},{56,2... | collective-permute-start | bytes 110600 | tf_op jit(solution)/shard_map/ppermute | solution.py:280
  44.9 2.2 %collective-permute-done.12.refs_3_ = f32[4,72,128]{2,1,0:T(8,128)S(1)} collective-permute-done((f32[4,72,128]{2,1,0:T(8,128)S(1)}, f32[4,72,128]{2,1,0:T(8,128)S(1)}, u32[]{:S(2)}, u32[]{:S(2)}) %collective-permute-start.12) | collective-permute-done | bytes 147488 | tf_op jit(solution)/shard_map/ppermute | solution.py:280
  47.3 0.9 %collective-permute-start.14 = (f32[72,128]{1,0:T(8,128)S(1)}, f32[72,128]{1,0:T(8,128)S(1)}, u32[]{:S(2)}, u32[]{:S(2)}) collective-permute-start(f32[72,128]{1,0:T(8,128)S(1)} %get-tuple-element.55), channel_id=1, source_target_pairs={{0,32},{8,40},{16,48},{24,56},{32,0},{40,8},{48,16},{56,24},{64,96... | collective-permute-start | bytes 110600 | tf_op jit(solution)/shard_map/ppermute | solution.py:280
  48.2 2.3 %collective-permute-start.15 = (f32[72,128]{1,0:T(8,128)S(1)}, f32[72,128]{1,0:T(8,128)S(1)}, u32[]{:S(2)}, u32[]{:S(2)}) collective-permute-start(f32[72,128]{1,0:T(8,128)S(1)} %get-tuple-element.56), channel_id=1, source_target_pairs={{0,48},{8,56},{16,0},{24,8},{32,16},{40,24},{48,32},{56,40},{64,11... | collective-permute-start | bytes 110600 | tf_op jit(solution)/shard_map/ppermute | solution.py:280
  50.5 1.9 %collective-permute-done.13.refs_5_ = f32[72,128]{1,0:T(8,128)S(1)} collective-permute-done((f32[72,128]{1,0:T(8,128)S(1)}, f32[72,128]{1,0:T(8,128)S(1)}, u32[]{:S(2)}, u32[]{:S(2)}) %collective-permute-start.13) | collective-permute-done | bytes 36896 | tf_op jit(solution)/shard_map/ppermute | solution.py:280
  52.8 0.9 %collective-permute-done.15.refs_7_ = f32[72,128]{1,0:T(8,128)S(1)} collective-permute-done((f32[72,128]{1,0:T(8,128)S(1)}, f32[72,128]{1,0:T(8,128)S(1)}, u32[]{:S(2)}, u32[]{:S(2)}) %collective-permute-start.15) | collective-permute-done | bytes 36896 | tf_op jit(solution)/shard_map/ppermute | solution.py:280
  53.7 1.3 %session.1 = (f32[16,512]{1,0:T(8,128)}, f32[16,512]{1,0:T(8,128)}, f32[144,128]{1,0:T(8,128)S(1)}) custom-call(s32[6]{0:T(128)S(1)} %stack.23.place, f32[72,128]{1,0:T(8,128)S(1)} %get-tuple-element.39.refs_0_, f32[72,128]{1,0:T(8,128)S(1)} %collective-permute-done.4.refs_1_, f32[72,128]{1,0:T(8,128)S(1)} %collective-permute-done.5.refs_2_, ...), custom_call_target="tpu_custom_call" | custom-call | tf_op jit(solution)/shard_map/session/pallas_call | solution.py:242
  55.0 1.9 %collective-permute-start.16 = (f32[144,128]{1,0:T(8,128)S(1)}, f32[144,128]{1,0:T(8,128)S(1)}, u32[]{:S(2)}, u32[]{:S(2)}) collective-permute-start(f32[144,128]{1,0:T(8,128)S(1)} %get-tuple-element.59.a_ref), channel_id=1, source_target_pairs={{0,1},{1,0},{2,3},{3,2},{4,5},{5,4},{6,7},{7,6},{8,9},{9,8},{10,11... | collective-permute-start | bytes 221192 | tf_op jit(solution)/shard_map/ppermute | solution.py:326
  56.9 2.4 %collective-permute-done.16.b_ref = f32[144,128]{1,0:T(8,128)S(1)} collective-permute-done((f32[144,128]{1,0:T(8,128)S(1)}, f32[144,128]{1,0:T(8,128)S(1)}, u32[]{:S(2)}, u32[]{:S(2)}) %collective-permute-start.16) | collective-permute-done | bytes 73760 | tf_op jit(solution)/shard_map/ppermute | solution.py:326
  59.4 4.0 %collective-permute-start.17 = (f32[144,128]{1,0:T(8,128)S(1)}, f32[144,128]{1,0:T(8,128)S(1)}, u32[]{:S(2)}, u32[]{:S(2)}) collective-permute-start(f32[144,128]{1,0:T(8,128)S(1)} %duo.2.a_ref), channel_id=1, source_target_pairs={{0,2},{1,3},{2,0},{3,1},{4,6},{5,7},{6,4},{7,5},{8,10},{9,11},{10,... | collective-permute-start | bytes 221192 | tf_op jit(solution)/shard_map/ppermute | solution.py:326
  63.4 2.3 %collective-permute-done.17.b_ref = f32[144,128]{1,0:T(8,128)S(1)} collective-permute-done((f32[144,128]{1,0:T(8,128)S(1)}, f32[144,128]{1,0:T(8,128)S(1)}, u32[]{:S(2)}, u32[]{:S(2)}) %collective-permute-start.17) | collective-permute-done | bytes 73760 | tf_op jit(solution)/shard_map/ppermute | solution.py:326
  65.7 6.2 %collective-permute-start.18 = (f32[144,128]{1,0:T(8,128)S(1)}, f32[144,128]{1,0:T(8,128)S(1)}, u32[]{:S(2)}, u32[]{:S(2)}) collective-permute-start(f32[144,128]{1,0:T(8,128)S(1)} %duo.3.a_ref), channel_id=1, source_target_pairs={{0,6},{1,7},{2,4},{3,5},{4,2},{5,3},{6,0},{7,1},{8,14},{9,15},{10,... | collective-permute-start | bytes 221192 | tf_op jit(solution)/shard_map/ppermute | solution.py:326
  72.0 2.4 %collective-permute-done.18.b_ref = f32[144,128]{1,0:T(8,128)S(1)} collective-permute-done((f32[144,128]{1,0:T(8,128)S(1)}, f32[144,128]{1,0:T(8,128)S(1)}, u32[]{:S(2)}, u32[]{:S(2)}) %collective-permute-start.18) | collective-permute-done | bytes 73760 | tf_op jit(solution)/shard_map/ppermute | solution.py:326
  74.3 1.3 %pooled.1 = (f32[16,512]{1,0:T(8,128)}, f32[16,512]{1,0:T(8,128)}) custom-call(s32[6]{0:T(128)S(1)} %stack.23.place, f32[144,128]{1,0:T(8,128)S(1)} %duo.3.a_ref, f32[144,128]{1,0:T(8,128)S(1)} %collective-permute-done.18.b_ref), custom_call_target="tpu_custom_call" | custom-call | tf_op jit(solution)/shard_map/pooled/pallas_call | solution.py:242
  (26 shorter events, 1.9 us)
Async XLA Ops:
  3.2 19.4 %collective-permute-start.7 = (bf16[1024,512]{1,0:T(8,128)(2,1)}, bf16[1024,512]{1,0:T(8,128)(2,1)S(1)}, u32[]{:S(2)}, u32[]{:S(2)}) collective-permute-start(bf16[1024,512]{1,0:T(8,128)(2,1)} %get-tuple-element.43), channel_id=1, source_target_pairs={{8,0},{16,8},{24,16},{32,24},{40,32},{48,40},{56,48},{64,56},{72,6... | collective-permute-start | bytes 3145736 | tf_op jit(solution)/shard_map/ppermute | solution.py:269
  7.8 18.2 %collective-permute-start.8 = (bf16[1024,512]{1,0:T(8,128)(2,1)S(1)}, bf16[1024,512]{1,0:T(8,128)(2,1)S(1)}, u32[]{:S(2)}, u32[]{:S(2)}) collective-permute-start(bf16[1024,512]{1,0:T(8,128)(2,1)S(1)} %get-tuple-element.44), channel_id=1, source_target_pairs={{0,8},{8,16},{16,24},{24,32},{32,40},{40,48},{48,56},{56,64},{64,7... | collective-permute-start | bytes 3145736 | tf_op jit(solution)/shard_map/ppermute | solution.py:270
  22.5 7.1 %collective-permute-start = (f32[4,4,72,128]{3,2,1,0:T(8,128)S(1)}, f32[4,4,72,128]{3,2,1,0:T(8,128)S(1)}, u32[]{:S(2)}, u32[]{:S(2)}) collective-permute-start(f32[4,4,72,128]{3,2,1,0:T(8,128)S(1)} %get-tuple-element.34), channel_id=1, source_target_pairs={{0,8},{8,0},{16,24},{24,16},{32,40},{40,32},{48,56},{56,48},{64,72... | collective-permute-start | bytes 1769480 | tf_op jit(solution)/shard_map/ppermute | solution.py:287
  29.5 3.5 %collective-permute-start.9 = (f32[4,4,72,128]{3,2,1,0:T(8,128)S(1)}, f32[4,4,72,128]{3,2,1,0:T(8,128)S(1)}, u32[]{:S(2)}, u32[]{:S(2)}) collective-permute-start(f32[4,4,72,128]{3,2,1,0:T(8,128)S(1)} %get-tuple-element.48), channel_id=1, source_target_pairs={{0,8},{8,0},{16,24},{24,16},{32,40},{40,32},{48,56},{56,48},{64,72... | collective-permute-start | bytes 1769480 | tf_op jit(solution)/shard_map/ppermute | solution.py:287
  29.7 10.7 %collective-permute-start.1 = (f32[4,72,128]{2,1,0:T(8,128)S(1)}, f32[4,72,128]{2,1,0:T(8,128)S(1)}, u32[]{:S(2)}, u32[]{:S(2)}) collective-permute-start(f32[4,72,128]{2,1,0:T(8,128)S(1)} %get-tuple-element.36), channel_id=1, source_target_pairs={{0,16},{8,24},{16,32},{24,40},{32,48},{40,56},{48,0},{56,8},{64,80... | collective-permute-start | bytes 442376 | tf_op jit(solution)/shard_map/ppermute | solution.py:280
  29.8 11.1 %collective-permute-start.2 = (f32[4,72,128]{2,1,0:T(8,128)S(1)}, f32[4,72,128]{2,1,0:T(8,128)S(1)}, u32[]{:S(2)}, u32[]{:S(2)}) collective-permute-start(f32[4,72,128]{2,1,0:T(8,128)S(1)} %get-tuple-element.37), channel_id=1, source_target_pairs={{0,32},{8,40},{16,48},{24,56},{32,0},{40,8},{48,16},{56,24},{64,96... | collective-permute-start | bytes 442376 | tf_op jit(solution)/shard_map/ppermute | solution.py:280
  29.9 11.1 %collective-permute-start.3 = (f32[4,72,128]{2,1,0:T(8,128)S(1)}, f32[4,72,128]{2,1,0:T(8,128)S(1)}, u32[]{:S(2)}, u32[]{:S(2)}) collective-permute-start(f32[4,72,128]{2,1,0:T(8,128)S(1)} %get-tuple-element.38), channel_id=1, source_target_pairs={{0,48},{8,56},{16,0},{24,8},{32,16},{40,24},{48,32},{56,40},{64,11... | collective-permute-start | bytes 442376 | tf_op jit(solution)/shard_map/ppermute | solution.py:280
  33.1 10.9 %collective-permute-start.10 = (f32[4,72,128]{2,1,0:T(8,128)S(1)}, f32[4,72,128]{2,1,0:T(8,128)S(1)}, u32[]{:S(2)}, u32[]{:S(2)}) collective-permute-start(f32[4,72,128]{2,1,0:T(8,128)S(1)} %get-tuple-element.50), channel_id=1, source_target_pairs={{0,64},{8,72},{16,80},{24,88},{32,96},{40,104},{48,112},{56,120},{... | collective-permute-start | bytes 442376 | tf_op jit(solution)/shard_map/ppermute | solution.py:280
  33.2 11.7 %collective-permute-start.11 = (f32[4,72,128]{2,1,0:T(8,128)S(1)}, f32[4,72,128]{2,1,0:T(8,128)S(1)}, u32[]{:S(2)}, u32[]{:S(2)}) collective-permute-start(f32[4,72,128]{2,1,0:T(8,128)S(1)} %get-tuple-element.51), channel_id=1, source_target_pairs={{0,128},{8,136},{16,144},{24,152},{32,160},{40,168},{48,176},{56,1... | collective-permute-start | bytes 442376 | tf_op jit(solution)/shard_map/ppermute | solution.py:280
  40.4 6.7 %collective-permute-start.12 = (f32[4,72,128]{2,1,0:T(8,128)S(1)}, f32[4,72,128]{2,1,0:T(8,128)S(1)}, u32[]{:S(2)}, u32[]{:S(2)}) collective-permute-start(f32[4,72,128]{2,1,0:T(8,128)S(1)} %get-tuple-element.52), channel_id=1, source_target_pairs={{0,192},{8,200},{16,208},{24,216},{32,224},{40,232},{48,240},{56,2... | collective-permute-start | bytes 442376 | tf_op jit(solution)/shard_map/ppermute | solution.py:280
  41.1 7.1 %collective-permute-start.4 = (f32[72,128]{1,0:T(8,128)S(1)}, f32[72,128]{1,0:T(8,128)S(1)}, u32[]{:S(2)}, u32[]{:S(2)}) collective-permute-start(f32[72,128]{1,0:T(8,128)S(1)} %get-tuple-element.40), channel_id=1, source_target_pairs={{0,64},{8,72},{16,80},{24,88},{32,96},{40,104},{48,112},{56,120},{... | collective-permute-start | bytes 110600 | tf_op jit(solution)/shard_map/ppermute | solution.py:280
  44.0 6.5 %collective-permute-start.5 = (f32[72,128]{1,0:T(8,128)S(1)}, f32[72,128]{1,0:T(8,128)S(1)}, u32[]{:S(2)}, u32[]{:S(2)}) collective-permute-start(f32[72,128]{1,0:T(8,128)S(1)} %get-tuple-element.41), channel_id=1, source_target_pairs={{0,128},{8,136},{16,144},{24,152},{32,160},{40,168},{48,176},{56,1... | collective-permute-start | bytes 110600 | tf_op jit(solution)/shard_map/ppermute | solution.py:280
  44.0 6.5 %collective-permute-start.6 = (f32[72,128]{1,0:T(8,128)S(1)}, f32[72,128]{1,0:T(8,128)S(1)}, u32[]{:S(2)}, u32[]{:S(2)}) collective-permute-start(f32[72,128]{1,0:T(8,128)S(1)} %get-tuple-element.42), channel_id=1, source_target_pairs={{0,192},{8,200},{16,208},{24,216},{32,224},{40,232},{48,240},{56,2... | collective-permute-start | bytes 110600 | tf_op jit(solution)/shard_map/ppermute | solution.py:280
  47.2 5.2 %collective-permute-start.13 = (f32[72,128]{1,0:T(8,128)S(1)}, f32[72,128]{1,0:T(8,128)S(1)}, u32[]{:S(2)}, u32[]{:S(2)}) collective-permute-start(f32[72,128]{1,0:T(8,128)S(1)} %get-tuple-element.54), channel_id=1, source_target_pairs={{0,16},{8,24},{16,32},{24,40},{32,48},{40,56},{48,0},{56,8},{64,80... | collective-permute-start | bytes 110600 | tf_op jit(solution)/shard_map/ppermute | solution.py:280
  47.3 5.5 %collective-permute-start.14 = (f32[72,128]{1,0:T(8,128)S(1)}, f32[72,128]{1,0:T(8,128)S(1)}, u32[]{:S(2)}, u32[]{:S(2)}) collective-permute-start(f32[72,128]{1,0:T(8,128)S(1)} %get-tuple-element.55), channel_id=1, source_target_pairs={{0,32},{8,40},{16,48},{24,56},{32,0},{40,8},{48,16},{56,24},{64,96... | collective-permute-start | bytes 110600 | tf_op jit(solution)/shard_map/ppermute | solution.py:280
  48.2 5.5 %collective-permute-start.15 = (f32[72,128]{1,0:T(8,128)S(1)}, f32[72,128]{1,0:T(8,128)S(1)}, u32[]{:S(2)}, u32[]{:S(2)}) collective-permute-start(f32[72,128]{1,0:T(8,128)S(1)} %get-tuple-element.56), channel_id=1, source_target_pairs={{0,48},{8,56},{16,0},{24,8},{32,16},{40,24},{48,32},{56,40},{64,11... | collective-permute-start | bytes 110600 | tf_op jit(solution)/shard_map/ppermute | solution.py:280
  55.0 4.4 %collective-permute-start.16 = (f32[144,128]{1,0:T(8,128)S(1)}, f32[144,128]{1,0:T(8,128)S(1)}, u32[]{:S(2)}, u32[]{:S(2)}) collective-permute-start(f32[144,128]{1,0:T(8,128)S(1)} %get-tuple-element.59.a_ref), channel_id=1, source_target_pairs={{0,1},{1,0},{2,3},{3,2},{4,5},{5,4},{6,7},{7,6},{8,9},{9,8},{10,11... | collective-permute-start | bytes 221192 | tf_op jit(solution)/shard_map/ppermute | solution.py:326
  59.4 6.3 %collective-permute-start.17 = (f32[144,128]{1,0:T(8,128)S(1)}, f32[144,128]{1,0:T(8,128)S(1)}, u32[]{:S(2)}, u32[]{:S(2)}) collective-permute-start(f32[144,128]{1,0:T(8,128)S(1)} %duo.2.a_ref), channel_id=1, source_target_pairs={{0,2},{1,3},{2,0},{3,1},{4,6},{5,7},{6,4},{7,5},{8,10},{9,11},{10,... | collective-permute-start | bytes 221192 | tf_op jit(solution)/shard_map/ppermute | solution.py:326
  65.7 8.6 %collective-permute-start.18 = (f32[144,128]{1,0:T(8,128)S(1)}, f32[144,128]{1,0:T(8,128)S(1)}, u32[]{:S(2)}, u32[]{:S(2)}) collective-permute-start(f32[144,128]{1,0:T(8,128)S(1)} %duo.3.a_ref), channel_id=1, source_target_pairs={{0,6},{1,7},{2,4},{3,5},{4,2},{5,3},{6,0},{7,1},{8,14},{9,15},{10,... | collective-permute-start | bytes 221192 | tf_op jit(solution)/shard_map/ppermute | solution.py:326

commit v3 on v2

v3 whole, which is shorter than its diff:
```python
import functools
import math

import jax
import jax.numpy as jnp
from jax import lax
from jax.experimental import pallas as pl
from jax.experimental.pallas import tpu as pltpu
from jax.sharding import PartitionSpec as P

LAG = 2048
BLK = 1024
LANES = 128
F32 = jnp.float32
CONTRACT = (((0,), (0,)), ((), ()))
VMEM_LIMIT = 47 * 1024 * 1024


def rows_below(limit, shape):
    return lax.broadcasted_iota(jnp.int32, shape, 0) < limit


def keep_below(block, limit):
    wide = jnp.where(rows_below(limit, block.shape), block.astype(F32), 0.0)
    return wide.astype(block.dtype)


def write_chunks(place, acc, tail, keep_ref, send_ref, x_first):
    core, my_x, my_y = place[0], place[4], place[5]
    side = keep_ref.shape[0]
    width = acc.shape[1]
    share = acc.shape[0] // (2 * side * side)
    for out, which in ((keep_ref, core), (send_ref, 1 - core)):
        for i in range(side):
            for j in range(side):
                far_x, far_y = (i, j) if x_first else (j, i)
                chip = lax.rem(my_x + far_x, side) * side + lax.rem(my_y + far_y, side)
                first = pl.multiple_of((2 * chip + which) * share, share)
                for col in range(width // LANES):
                    out[i, j, col * share : (col + 1) * share, :] = acc[
                        pl.ds(first, share), col * LANES : (col + 1) * LANES
                    ]
                out[i, j, share * (width // LANES) :, :] = tail


def tail_rows(sums, valid):
    width = sums.shape[1]
    parts = [sums[:, c * LANES : (c + 1) * LANES] for c in range(width // LANES)]
    count = jnp.full((8 - len(parts), LANES), valid, jnp.int32).astype(F32)
    return jnp.concatenate([*parts, count], axis=0)


def fold(wide):
    return jnp.sum(wide.reshape(-1, 8, wide.shape[1]), axis=0)


def dot(early, late):
    return lax.dot_general(early, late, CONTRACT, preferred_element_type=F32)


def add_whole(block_ref, first, acc, sums, pair):
    block = block_ref[...]
    acc[...] += dot(block, block)
    if pair is not None:
        pair[0][...] += dot(pair[1][...], block)
    total = fold(block.astype(F32))
    sums[0:8, :] += total
    sums[8:16, :] += total * jnp.where(first >= LAG, 1.0, 0.0)


def add_block(block_ref, first, count, acc, sums, pair):
    full = first + BLK <= count

    @pl.when(full)
    def _():
        add_whole(block_ref, first, acc, sums, pair)

    @pl.when(jnp.logical_and(jnp.logical_not(full), first < count + LAG))
    def _():
        block = block_ref[...]
        wide = block.astype(F32)
        held = jnp.where(rows_below(count - first, wide.shape), wide, 0.0)
        acc[...] += dot(held.astype(block.dtype), block)
        if pair is not None:
            pair[0][...] += dot(keep_below(pair[1][...], count - first + LAG), block)
        later = jnp.where(rows_below(count + LAG - first, wide.shape), wide, 0.0)
        sums[0:8, :] += fold(held)
        sums[8:16, :] += fold(later) * jnp.where(first >= LAG, 1.0, 0.0)


def edge_kernel(which, place, x_hbm, out_ref, sems):
    rows, height = x_hbm.shape[0], out_ref.shape[0]
    parts = sems.shape[0]
    step = height // parts
    start = jnp.where(place[0] == which, rows - height, 0)
    copies = []
    for k in range(parts):
        first = pl.multiple_of(start + k * step, step)
        source = x_hbm.at[pl.ds(first, step)]
        copies.append(pltpu.make_async_copy(source, out_ref.at[pl.ds(k * step, step)], sems.at[k]))
    for copy in copies:
        copy.start()
    for copy in copies:
        copy.wait()


def moments_kernel(
    place, x_hbm, keep_ref, send_ref, lag, sum_y_ref, second_ref, late_ref, xs, acc, sums, sems
):
    base, count = place[1], place[2]
    rows = x_hbm.shape[0]
    blocks = rows // BLK
    ahead = LAG // BLK

    def copy(b):
        return pltpu.make_async_copy(x_hbm.at[pl.ds(b * BLK, BLK)], xs.at[b], sems.at[b])

    def again(k, b, out):
        return pltpu.make_async_copy(x_hbm.at[pl.ds(b * BLK, BLK)], out, sems.at[blocks + k])

    kept = [again(0, 1, second_ref), again(1, blocks - ahead, late_ref)]
    for b in range(blocks):
        copy(b).start()
    for each in kept:
        each.start()
    acc[...] = jnp.zeros_like(acc)
    sums[...] = jnp.zeros_like(sums)
    lag[...] = jnp.zeros_like(lag)

    def step(b, with_pair):
        copy(b).wait()
        pair = (lag, xs.at[b - ahead]) if with_pair else None
        add_block(xs.at[b], base + b * BLK, count, acc, sums, pair)

    pl.loop(0, ahead)(lambda b: step(b, False))
    pl.loop(ahead, blocks)(lambda b: step(b, True))
    for each in kept:
        each.wait()
    valid = jnp.clip(count - base, 0, rows)
    sum_x = jnp.sum(sums[0:8, :], axis=0, keepdims=True)
    sum_y = jnp.sum(sums[8:16, :], axis=0, keepdims=True)
    write_chunks(place, acc, tail_rows(sum_x, valid), keep_ref, send_ref, True)
    sum_y_ref[...] = jnp.broadcast_to(sum_y, sum_y_ref.shape)


def border_kernel(
    place, far_ref, near_ref, second_ref, late_ref, part_ref, sum_y_ref, keep_ref, send_ref, acc
):
    core, base, count = place[0], place[1], place[2]
    rows = place[6]
    first = base + rows - LAG

    def add(next_ref, last_ref):
        full = first + BLK <= count

        @pl.when(full)
        def _():
            acc[...] = (
                part_ref[...] + dot(late_ref[...], next_ref[...]) + dot(last_ref[...], second_ref[...])
            )

        @pl.when(jnp.logical_not(full))
        def _():
            early = keep_below(late_ref[...], count - first)
            before = keep_below(last_ref[...], count - base + BLK)
            acc[...] = part_ref[...] + dot(early, next_ref[...]) + dot(before, second_ref[...])

    @pl.when(core == 1)
    def _():
        add(far_ref, near_ref)

    @pl.when(core == 0)
    def _():
        add(near_ref, far_ref)

    valid = jnp.clip(count - base, 0, rows)
    write_chunks(place, acc, tail_rows(sum_y_ref[0:1, :], valid), keep_ref, send_ref, False)


def pair_kernel(keep_ref, met_ref, *outs):
    for d, out in enumerate(outs):
        out[...] = keep_ref[d] + met_ref[d]


def line_kernel(*refs):
    side = len(refs) // 2
    ins, outs = refs[:side], refs[side:]
    for d, out in enumerate(outs):
        out[...] = (ins[0][d] + ins[1][d]) + (ins[2][d] + ins[3][d])


def row_of(rows):
    return jnp.concatenate([rows[c : c + 1, :] for c in range(rows.shape[0])], axis=1)


def centered(total, mean_rows, mean_cols, number, share, out_ref):
    for col in range(out_ref.shape[1] // LANES):
        lanes = slice(col * LANES, (col + 1) * LANES)
        block = total[col * share : (col + 1) * share, :]
        out_ref[:, lanes] = block / number - mean_rows * mean_cols[:, lanes]


def finish(total_i, total_l, first_row, inst_ref, lag_ref):
    share, width = inst_ref.shape
    cols = width // LANES
    tail = share * cols
    number = total_i[tail + cols : tail + cols + 1, 0:1]
    mean_x = row_of(total_i[tail : tail + cols, :]) / number
    mean_y = row_of(total_l[tail : tail + cols, :]) / number
    row = lax.broadcasted_iota(jnp.int32, (share, width), 0)
    col = lax.broadcasted_iota(jnp.int32, (share, width), 1)
    own = jnp.where(col == row + first_row, jnp.broadcast_to(mean_x, (share, width)), 0.0)
    mean_rows = jnp.sum(own, axis=1, keepdims=True)
    centered(total_i, mean_rows, mean_x, number, share, inst_ref)
    centered(total_l, mean_rows, mean_y, number, share, lag_ref)


def plane_kernel(*refs):
    *parts, total_ref = refs
    half = total_ref.shape[0] // 2
    side = len(parts) // 2
    for k in range(2):
        a, b, c, d = parts[k * side : (k + 1) * side]
        total_ref[k * half : (k + 1) * half, :] = (a[...] + b[...]) + (c[...] + d[...])


def session_kernel(place, total_ref, inst_ref, lag_ref):
    half = total_ref.shape[0] // 2
    finish(total_ref[:half], total_ref[half:], place[3], inst_ref, lag_ref)


def duo_kernel(a_ref, b_ref, out_ref):
    out_ref[...] = a_ref[...] + b_ref[...]


def pooled_kernel(place, a_ref, b_ref, inst_ref, lag_ref):
    total = a_ref[...] + b_ref[...]
    half = total.shape[0] // 2
    finish(total[:half], total[half:], place[3], inst_ref, lag_ref)


def on_device(frames, pair_count):
    local = frames[0]
    rows, width = local.shape
    blocks = rows // BLK
    parts = lax.axis_size("tm")
    sessions = lax.axis_size("group")
    side = math.isqrt(parts // 2)
    share = width // parts
    chunk = share * (width // LANES) + 8
    me = lax.axis_index("tm")
    numbers = [me % 2, me * rows, pair_count[0], me * share, me // (2 * side), (me // 2) % side, rows]
    place = jnp.stack(numbers).astype(jnp.int32)

    smem = pl.BlockSpec(memory_space=pltpu.SMEM)
    vmem = pl.BlockSpec(memory_space=pltpu.VMEM)
    hbm = pl.BlockSpec(memory_space=pl.ANY)
    params = pltpu.CompilerParams(vmem_limit_bytes=VMEM_LIMIT)

    def floats(*shape):
        return jax.ShapeDtypeStruct(shape, F32)

    def call(kernel, name, ins, out_shape, scratch=(), flops=0, moved=0):
        specs = jax.tree.map(lambda _: vmem, out_shape)
        return pl.pallas_call(
            kernel,
            out_shape=out_shape,
            in_specs=[spec for _, spec in ins],
            out_specs=specs,
            scratch_shapes=list(scratch),
            compiler_params=params,
            cost_estimate=pl.CostEstimate(flops=flops, bytes_accessed=moved, transcendentals=0),
            name=name,
        )(*[operand for operand, _ in ins])

    def dma(n):
        return pltpu.SemaphoreType.DMA((n,))

    where, frames_in = (place, smem), (local, hbm)
    edge = jax.ShapeDtypeStruct((BLK, width), local.dtype)
    swap = [(i, i ^ 1) for i in range(parts)]
    cross = [(i, i + 1 if i % 2 else i - 1) for i in range(1, parts - 1)]

    def neighbours(which, route, name):
        kernel = functools.partial(edge_kernel, which)
        block = call(kernel, name, [where, frames_in], edge, [dma(4)], 0, 2 * BLK * width)
        return lax.ppermute(block, "tm", route)

    far = neighbours(1, cross, "edge_far")
    near = neighbours(0, swap, "edge_near")

    def at(x, y, c):
        return ((x % side) * side + y % side) * 2 + c

    def along(block, far_x, far_y):
        grid = [(x, y, c) for x in range(side) for y in range(side) for c in range(2)]
        route = [(at(x, y, c), at(x + far_x, y + far_y, c)) for x, y, c in grid]
        return lax.ppermute(block, "tm", route)

    def gather(blocks, on_x):
        moved = [along(blocks[d], d * on_x, d * (1 - on_x)) for d in range(1, side)]
        return [blocks[0], *moved]

    def over_pair(keep, send, name):
        met = lax.ppermute(send, "tm", swap)
        return call(pair_kernel, "pair_" + name, [(keep, vmem), (met, vmem)], [floats(side, chunk, LANES)] * side)

    def over_plane(lines, x_first, name):
        came = gather(lines, x_first)
        cells = call(line_kernel, "line_" + name, [(v, vmem) for v in came], [floats(chunk, LANES)] * side)
        return gather(cells, 1 - x_first)

    half = floats(side, side, chunk, LANES)
    square = pltpu.VMEM((width, width), F32)
    held = pltpu.VMEM((blocks, BLK, width), local.dtype)
    work = 2 * rows * width * width
    keep_i, send_i, partial, sum_y, second, late = call(
        moments_kernel,
        "moments",
        [where, frames_in],
        (half, half, floats(width, width), floats(8, width), edge, edge),
        [held, square, pltpu.VMEM((16, width), F32), dma(blocks + 2)],
        work * 7 // 4,
        rows * width * 2,
    )
    keep_l, send_l = call(
        border_kernel,
        "border",
        [where, *[(v, vmem) for v in (far, near, second, late, partial, sum_y)]],
        (half, half),
        [square],
        work // 4,
        rows * width,
    )
    lines_i = over_pair(keep_i, send_i, "instant")
    cells_i = over_plane(lines_i, 1, "instant")
    cells_l = over_plane(over_pair(keep_l, send_l, "lagged"), 0, "lagged")
    out = floats(share, width)
    total = call(plane_kernel, "plane", [(v, vmem) for v in (*cells_i, *cells_l)], floats(2 * chunk, LANES))
    group_instant, group_lagged = call(session_kernel, "session", [where, (total, vmem)], (out, out))
    for route in (lambda i: i ^ 1, lambda i: i ^ 2, lambda i: (sessions - 2 - (i & -2)) | (i & 1)):
        other = lax.ppermute(total, "group", [(i, route(i)) for i in range(sessions)])
        last = (total, other)
        total = call(duo_kernel, "duo", [(v, vmem) for v in last], floats(2 * chunk, LANES))
    pooled_instant, pooled_lagged = call(
        pooled_kernel, "pooled", [where, *[(v, vmem) for v in last]], (out, out)
    )
    return (group_instant[None], group_lagged[None], pooled_instant, pooled_lagged)


def solution(mesh):
    in_specs = (P("group", "tm", None), P("group"))
    out_specs = (P("group", "tm", None), P("group", "tm", None), P("tm", None), P("tm", None))
    return jax.shard_map(
        on_device, mesh=mesh, in_specs=in_specs, out_specs=out_specs, check_vma=False
    )
```

time: 76.1 us -> 68.6 us (0.901)
  waiting for transfers between devices: 20.7 us -> 15.2 us
  Pallas kernels: 20.9 us -> 19.6 us
    ppermute x4, waiting for transfers between devices: 3.44 us -> 0.01 us  [the longest x2 0.01 us: neighbours(): return lax.ppermute(block, 'tm', route)]
    pallas_call x1 -> x0, Pallas kernels: 2.57 us -> none  [on_device(): pl.pallas_call(edges_kernel, out_shape=(edge, edge), in_specs=[hbm], out_...]
    ppermute x12, waiting for transfers between devices: 10.1 us -> 7.86 us  [along(): return lax.ppermute(block, 'tm', route)]
    ppermute x12, starting transfers between devices: 13.7 us -> 15.6 us  [along(): return lax.ppermute(block, 'tm', route)]
    ppermute x4, starting transfers between devices: 6.73 us -> 5.42 us  [the longest x2 4.72 us: neighbours(): return lax.ppermute(block, 'tm', route)]
    pallas_call x10 -> x13, Pallas kernels: 18.3 us -> 19.6 us  [call(): pl.pallas_call(kernel, out_shape=out_shape, in_specs=[spec for _, spec in...]
    ppermute x3, starting transfers between devices: 12.1 us -> 11.2 us  [on_device(): lax.ppermute(total, 'group', [(i, route(i)) for i in range(sessions)])]
  transfers between devices with their start and end apart: 19 -> 19, of which waited for: 10 -> 9; matrix products, arithmetic and copies ran while one was open for 0% -> 0% of each run, Pallas kernels for 21% -> 24%
where the time goes in v3:
time: 68.6 us; the launch traced here: 68.5 us
  starting transfers between devices  32.2 us (47%)
  Pallas kernels  19.6 us (29%)
  waiting for transfers between devices  15.2 us (22%)
  between operations  1.42 us (2%)
    pallas_call x13, Pallas kernels, call(): pl.pallas_call(kernel, out_shape=out_shape, in_specs=[spec for _, spec in...  19.6 us
    ppermute x12, starting transfers between devices, along(): return lax.ppermute(block, 'tm', route)  15.6 us
    ppermute x3, starting transfers between devices, on_device(): lax.ppermute(total, 'group', [(i, route(i)) for i in range(sessions)])  11.2 us
    ppermute x12, waiting for transfers between devices, along(): return lax.ppermute(block, 'tm', route)  7.86 us
    ppermute x3, waiting for transfers between devices, on_device(): lax.ppermute(total, 'group', [(i, route(i)) for i in range(sessions)])  7.37 us
    ppermute x2, starting transfers between devices, neighbours(): return lax.ppermute(block, 'tm', route)  4.72 us
  transfers between devices with their start and end apart: 19, of which 9 were waited for; matrix products, arithmetic and copies ran while one was open for 0% of the time, Pallas kernels for 24%

profile of v3, /device:TPU:6, one launch (start us, length us, event | category | flops | bytes accessed | tf_op | source)
XLA Modules:
  0.0 68.5 jit_solution(13634026922714696241)
XLA Ops:
  1.4 1.8 %edge_far.1 = bf16[1024,512]{1,0:T(8,128)(2,1)S(1)} custom-call(s32[7]{0:T(128)S(1)} %stack.23.place, bf16[8192,512]{1,0:T(8,128)(2,1)} %bitcast.8), custom_call_target="tpu_custom_call" | custom-call | bytes 1048576 | tf_op jit(solution)/shard_map/edge_far/pallas_call | solution.py:265
  3.2 4.6 %collective-permute-start.7 = (bf16[1024,512]{1,0:T(8,128)(2,1)S(1)}, bf16[1024,512]{1,0:T(8,128)(2,1)S(1)}, u32[]{:S(2)}, u32[]{:S(2)}) collective-permute-start(bf16[1024,512]{1,0:T(8,128)(2,1)S(1)} %edge_far.1), channel_id=1, source_target_pairs={{8,16},{16,8},{24,32},{32,24},{40,48},{48,40},{56,64},{64,56},{72,... | collective-permute-start | bytes 3145736 | tf_op jit(solution)/shard_map/ppermute | solution.py:287
  7.8 1.8 %edge_near.1 = bf16[1024,512]{1,0:T(8,128)(2,1)S(1)} custom-call(s32[7]{0:T(128)S(1)} %stack.23.place, bf16[8192,512]{1,0:T(8,128)(2,1)} %bitcast.9), custom_call_target="tpu_custom_call" | custom-call | bytes 1048576 | tf_op jit(solution)/shard_map/edge_near/pallas_call | solution.py:265
  9.7 11.2 %moments.1 = (f32[4,4,72,128]{3,2,1,0:T(8,128)S(1)}, f32[4,4,72,128]{3,2,1,0:T(8,128)S(1)}, f32[512,512]{1,0:T(8,128)S(1)}, f32[8,512]{1,0:T(8,128)S(1)}, bf16[1...) custom-call(s32[7]{0:T(128)S(1)} %stack.23.place, bf16[8192,512]{1,0:T(8,128)(2,1)} %bitcast.10), custom_call_target="tpu_custom_call" | custom-call | flops 7516192768 | bytes 8388608 | tf_op jit(solution)/shard_map/moments/pallas_call | solution.py:265
  20.9 0.6 collective-permute-start
  21.5 1.9 %border.1 = (f32[4,4,72,128]{3,2,1,0:T(8,128)S(1)}, f32[4,4,72,128]{3,2,1,0:T(8,128)S(1)}) custom-call(s32[7]{0:T(128)S(1)} %stack.23.place, bf16[1024,512]{1,0:T(8,128)(2,1)S(1)} %collective-permute-done.7.far_ref, bf16[1024,512]{1,0:T(8,128)(2,1)S(1)} %collective-permute-done.8.near_ref, bf16[1024,512]{1,0:T(8,128)(2,1)S(1)} %get-tuple-element.42.second_ref, ...), custom_call_target="tpu_custom_call" | custom-call | flops 1073741824 | bytes 4194304 | tf_op jit(solution)/shard_map/border/pallas_call | solution.py:265
  23.7 2.8 %collective-permute-start.2 = (f32[4,72,128]{2,1,0:T(8,128)S(1)}, f32[4,72,128]{2,1,0:T(8,128)S(1)}, u32[]{:S(2)}, u32[]{:S(2)}) collective-permute-start(f32[4,72,128]{2,1,0:T(8,128)S(1)} %get-tuple-element.36), channel_id=1, source_target_pairs={{0,128},{8,136},{16,144},{24,152},{32,160},{40,168},{48,176},{56,1... | collective-permute-start | bytes 442376 | tf_op jit(solution)/shard_map/ppermute | solution.py:298
  26.6 0.7 %collective-permute-start.10 = (f32[4,72,128]{2,1,0:T(8,128)S(1)}, f32[4,72,128]{2,1,0:T(8,128)S(1)}, u32[]{:S(2)}, u32[]{:S(2)}) collective-permute-start(f32[4,72,128]{2,1,0:T(8,128)S(1)} %get-tuple-element.49), channel_id=1, source_target_pairs={{0,16},{8,24},{16,32},{24,40},{32,48},{40,56},{48,0},{56,8},{64,80... | collective-permute-start | bytes 442376 | tf_op jit(solution)/shard_map/ppermute | solution.py:298
  27.3 3.6 %collective-permute-start.11 = (f32[4,72,128]{2,1,0:T(8,128)S(1)}, f32[4,72,128]{2,1,0:T(8,128)S(1)}, u32[]{:S(2)}, u32[]{:S(2)}) collective-permute-start(f32[4,72,128]{2,1,0:T(8,128)S(1)} %get-tuple-element.50), channel_id=1, source_target_pairs={{0,32},{8,40},{16,48},{24,56},{32,0},{40,8},{48,16},{56,24},{64,96... | collective-permute-start | bytes 442376 | tf_op jit(solution)/shard_map/ppermute | solution.py:298
  30.9 1.0 %collective-permute-start.12 = (f32[4,72,128]{2,1,0:T(8,128)S(1)}, f32[4,72,128]{2,1,0:T(8,128)S(1)}, u32[]{:S(2)}, u32[]{:S(2)}) collective-permute-start(f32[4,72,128]{2,1,0:T(8,128)S(1)} %get-tuple-element.51), channel_id=1, source_target_pairs={{0,48},{8,56},{16,0},{24,8},{32,16},{40,24},{48,32},{56,40},{64,11... | collective-permute-start | bytes 442376 | tf_op jit(solution)/shard_map/ppermute | solution.py:298
  32.0 2.7 %collective-permute-done.3.refs_3_ = f32[4,72,128]{2,1,0:T(8,128)S(1)} collective-permute-done((f32[4,72,128]{2,1,0:T(8,128)S(1)}, f32[4,72,128]{2,1,0:T(8,128)S(1)}, u32[]{:S(2)}, u32[]{:S(2)}) %collective-permute-start.3) | collective-permute-done | bytes 147488 | tf_op jit(solution)/shard_map/ppermute | solution.py:298
  35.0 3.6 %collective-permute-start.5 = (f32[72,128]{1,0:T(8,128)S(1)}, f32[72,128]{1,0:T(8,128)S(1)}, u32[]{:S(2)}, u32[]{:S(2)}) collective-permute-start(f32[72,128]{1,0:T(8,128)S(1)} %get-tuple-element.40), channel_id=1, source_target_pairs={{0,32},{8,40},{16,48},{24,56},{32,0},{40,8},{48,16},{56,24},{64,96... | collective-permute-start | bytes 110600 | tf_op jit(solution)/shard_map/ppermute | solution.py:298
  39.0 2.2 %collective-permute-start.13 = (f32[72,128]{1,0:T(8,128)S(1)}, f32[72,128]{1,0:T(8,128)S(1)}, u32[]{:S(2)}, u32[]{:S(2)}) collective-permute-start(f32[72,128]{1,0:T(8,128)S(1)} %get-tuple-element.53), channel_id=1, source_target_pairs={{0,64},{8,72},{16,80},{24,88},{32,96},{40,104},{48,112},{56,120},{... | collective-permute-start | bytes 110600 | tf_op jit(solution)/shard_map/ppermute | solution.py:298
  41.2 0.9 %collective-permute-start.14 = (f32[72,128]{1,0:T(8,128)S(1)}, f32[72,128]{1,0:T(8,128)S(1)}, u32[]{:S(2)}, u32[]{:S(2)}) collective-permute-start(f32[72,128]{1,0:T(8,128)S(1)} %get-tuple-element.54), channel_id=1, source_target_pairs={{0,128},{8,136},{16,144},{24,152},{32,160},{40,168},{48,176},{56,1... | collective-permute-start | bytes 110600 | tf_op jit(solution)/shard_map/ppermute | solution.py:298
  43.0 3.6 %collective-permute-done.14.refs_6_ = f32[72,128]{1,0:T(8,128)S(1)} collective-permute-done((f32[72,128]{1,0:T(8,128)S(1)}, f32[72,128]{1,0:T(8,128)S(1)}, u32[]{:S(2)}, u32[]{:S(2)}) %collective-permute-start.14) | collective-permute-done | bytes 36896 | tf_op jit(solution)/shard_map/ppermute | solution.py:298
  46.7 0.6 collective-permute-done.15.refs_7_
  47.3 2.0 %collective-permute-start.16 = (f32[144,128]{1,0:T(8,128)S(1)}, f32[144,128]{1,0:T(8,128)S(1)}, u32[]{:S(2)}, u32[]{:S(2)}) collective-permute-start(f32[144,128]{1,0:T(8,128)S(1)} %plane.1.total_ref.a_ref), channel_id=1, source_target_pairs={{0,1},{1,0},{2,3},{3,2},{4,5},{5,4},{6,7},{7,6},{8,9},{9,8},{10,11... | collective-permute-start | bytes 221192 | tf_op jit(solution)/shard_map/ppermute | solution.py:342
  49.3 3.2 %collective-permute-done.16.b_ref = f32[144,128]{1,0:T(8,128)S(1)} collective-permute-done((f32[144,128]{1,0:T(8,128)S(1)}, f32[144,128]{1,0:T(8,128)S(1)}, u32[]{:S(2)}, u32[]{:S(2)}) %collective-permute-start.16) | collective-permute-done | bytes 73760 | tf_op jit(solution)/shard_map/ppermute | solution.py:342
  52.5 2.6 %collective-permute-start.17 = (f32[144,128]{1,0:T(8,128)S(1)}, f32[144,128]{1,0:T(8,128)S(1)}, u32[]{:S(2)}, u32[]{:S(2)}) collective-permute-start(f32[144,128]{1,0:T(8,128)S(1)} %duo.2.a_ref), channel_id=1, source_target_pairs={{0,2},{1,3},{2,0},{3,1},{4,6},{5,7},{6,4},{7,5},{8,10},{9,11},{10,... | collective-permute-start | bytes 221192 | tf_op jit(solution)/shard_map/ppermute | solution.py:342
  55.1 2.8 %collective-permute-done.17.b_ref = f32[144,128]{1,0:T(8,128)S(1)} collective-permute-done((f32[144,128]{1,0:T(8,128)S(1)}, f32[144,128]{1,0:T(8,128)S(1)}, u32[]{:S(2)}, u32[]{:S(2)}) %collective-permute-start.17) | collective-permute-done | bytes 73760 | tf_op jit(solution)/shard_map/ppermute | solution.py:342
  57.9 6.6 %collective-permute-start.18 = (f32[144,128]{1,0:T(8,128)S(1)}, f32[144,128]{1,0:T(8,128)S(1)}, u32[]{:S(2)}, u32[]{:S(2)}) collective-permute-start(f32[144,128]{1,0:T(8,128)S(1)} %duo.3.a_ref), channel_id=1, source_target_pairs={{0,6},{1,7},{2,4},{3,5},{4,2},{5,3},{6,0},{7,1},{8,14},{9,15},{10,... | collective-permute-start | bytes 221192 | tf_op jit(solution)/shard_map/ppermute | solution.py:342
  64.5 1.3 %session.1 = (f32[16,512]{1,0:T(8,128)}, f32[16,512]{1,0:T(8,128)}) custom-call(s32[7]{0:T(128)S(1)} %stack.23.place, f32[144,128]{1,0:T(8,128)S(1)} %plane.1.total_ref.a_ref), custom_call_target="tpu_custom_call" | custom-call | tf_op jit(solution)/shard_map/session/pallas_call | solution.py:265
  65.8 1.4 %collective-permute-done.18.b_ref = f32[144,128]{1,0:T(8,128)S(1)} collective-permute-done((f32[144,128]{1,0:T(8,128)S(1)}, f32[144,128]{1,0:T(8,128)S(1)}, u32[]{:S(2)}, u32[]{:S(2)}) %collective-permute-start.18) | collective-permute-done | bytes 73760 | tf_op jit(solution)/shard_map/ppermute | solution.py:342
  67.2 1.3 %pooled.1 = (f32[16,512]{1,0:T(8,128)}, f32[16,512]{1,0:T(8,128)}) custom-call(s32[7]{0:T(128)S(1)} %stack.23.place, f32[144,128]{1,0:T(8,128)S(1)} %duo.3.a_ref, f32[144,128]{1,0:T(8,128)S(1)} %collective-permute-done.18.b_ref), custom_call_target="tpu_custom_call" | custom-call | tf_op jit(solution)/shard_map/pooled/pallas_call | solution.py:265
  (28 shorter events, 2.2 us)
Async XLA Ops:
  3.2 18.3 %collective-permute-start.7 = (bf16[1024,512]{1,0:T(8,128)(2,1)S(1)}, bf16[1024,512]{1,0:T(8,128)(2,1)S(1)}, u32[]{:S(2)}, u32[]{:S(2)}) collective-permute-start(bf16[1024,512]{1,0:T(8,128)(2,1)S(1)} %edge_far.1), channel_id=1, source_target_pairs={{8,16},{16,8},{24,32},{32,24},{40,48},{48,40},{56,64},{64,56},{72,... | collective-permute-start | bytes 3145736 | tf_op jit(solution)/shard_map/ppermute | solution.py:287
  9.6 11.9 %collective-permute-start.8 = (bf16[1024,512]{1,0:T(8,128)(2,1)S(1)}, bf16[1024,512]{1,0:T(8,128)(2,1)S(1)}, u32[]{:S(2)}, u32[]{:S(2)}) collective-permute-start(bf16[1024,512]{1,0:T(8,128)(2,1)S(1)} %edge_near.1), channel_id=1, source_target_pairs={{0,8},{8,0},{16,24},{24,16},{32,40},{40,32},{48,56},{56,48},{64,72... | collective-permute-start | bytes 3145736 | tf_op jit(solution)/shard_map/ppermute | solution.py:287
  20.9 2.6 %collective-permute-start = (f32[4,4,72,128]{3,2,1,0:T(8,128)S(1)}, f32[4,4,72,128]{3,2,1,0:T(8,128)S(1)}, u32[]{:S(2)}, u32[]{:S(2)}) collective-permute-start(f32[4,4,72,128]{3,2,1,0:T(8,128)S(1)} %get-tuple-element.33), channel_id=1, source_target_pairs={{0,8},{8,0},{16,24},{24,16},{32,40},{40,32},{48,56},{56,48},{64,72... | collective-permute-start | bytes 1769480 | tf_op jit(solution)/shard_map/ppermute | solution.py:305
  23.5 3.0 %collective-permute-start.9 = (f32[4,4,72,128]{3,2,1,0:T(8,128)S(1)}, f32[4,4,72,128]{3,2,1,0:T(8,128)S(1)}, u32[]{:S(2)}, u32[]{:S(2)}) collective-permute-start(f32[4,4,72,128]{3,2,1,0:T(8,128)S(1)} %get-tuple-element.47), channel_id=1, source_target_pairs={{0,8},{8,0},{16,24},{24,16},{32,40},{40,32},{48,56},{56,48},{64,72... | collective-permute-start | bytes 1769480 | tf_op jit(solution)/shard_map/ppermute | solution.py:305
  23.6 7.3 %collective-permute-start.1 = (f32[4,72,128]{2,1,0:T(8,128)S(1)}, f32[4,72,128]{2,1,0:T(8,128)S(1)}, u32[]{:S(2)}, u32[]{:S(2)}) collective-permute-start(f32[4,72,128]{2,1,0:T(8,128)S(1)} %get-tuple-element.35), channel_id=1, source_target_pairs={{0,64},{8,72},{16,80},{24,88},{32,96},{40,104},{48,112},{56,120},{... | collective-permute-start | bytes 442376 | tf_op jit(solution)/shard_map/ppermute | solution.py:298
  23.7 8.2 %collective-permute-start.2 = (f32[4,72,128]{2,1,0:T(8,128)S(1)}, f32[4,72,128]{2,1,0:T(8,128)S(1)}, u32[]{:S(2)}, u32[]{:S(2)}) collective-permute-start(f32[4,72,128]{2,1,0:T(8,128)S(1)} %get-tuple-element.36), channel_id=1, source_target_pairs={{0,128},{8,136},{16,144},{24,152},{32,160},{40,168},{48,176},{56,1... | collective-permute-start | bytes 442376 | tf_op jit(solution)/shard_map/ppermute | solution.py:298
  26.5 8.2 %collective-permute-start.3 = (f32[4,72,128]{2,1,0:T(8,128)S(1)}, f32[4,72,128]{2,1,0:T(8,128)S(1)}, u32[]{:S(2)}, u32[]{:S(2)}) collective-permute-start(f32[4,72,128]{2,1,0:T(8,128)S(1)} %get-tuple-element.37), channel_id=1, source_target_pairs={{0,192},{8,200},{16,208},{24,216},{32,224},{40,232},{48,240},{56,2... | collective-permute-start | bytes 442376 | tf_op jit(solution)/shard_map/ppermute | solution.py:298
  26.6 12.1 %collective-permute-start.10 = (f32[4,72,128]{2,1,0:T(8,128)S(1)}, f32[4,72,128]{2,1,0:T(8,128)S(1)}, u32[]{:S(2)}, u32[]{:S(2)}) collective-permute-start(f32[4,72,128]{2,1,0:T(8,128)S(1)} %get-tuple-element.49), channel_id=1, source_target_pairs={{0,16},{8,24},{16,32},{24,40},{32,48},{40,56},{48,0},{56,8},{64,80... | collective-permute-start | bytes 442376 | tf_op jit(solution)/shard_map/ppermute | solution.py:298
  27.3 11.7 %collective-permute-start.11 = (f32[4,72,128]{2,1,0:T(8,128)S(1)}, f32[4,72,128]{2,1,0:T(8,128)S(1)}, u32[]{:S(2)}, u32[]{:S(2)}) collective-permute-start(f32[4,72,128]{2,1,0:T(8,128)S(1)} %get-tuple-element.50), channel_id=1, source_target_pairs={{0,32},{8,40},{16,48},{24,56},{32,0},{40,8},{48,16},{56,24},{64,96... | collective-permute-start | bytes 442376 | tf_op jit(solution)/shard_map/ppermute | solution.py:298
  30.9 8.0 %collective-permute-start.12 = (f32[4,72,128]{2,1,0:T(8,128)S(1)}, f32[4,72,128]{2,1,0:T(8,128)S(1)}, u32[]{:S(2)}, u32[]{:S(2)}) collective-permute-start(f32[4,72,128]{2,1,0:T(8,128)S(1)} %get-tuple-element.51), channel_id=1, source_target_pairs={{0,48},{8,56},{16,0},{24,8},{32,16},{40,24},{48,32},{56,40},{64,11... | collective-permute-start | bytes 442376 | tf_op jit(solution)/shard_map/ppermute | solution.py:298
  34.8 7.4 %collective-permute-start.4 = (f32[72,128]{1,0:T(8,128)S(1)}, f32[72,128]{1,0:T(8,128)S(1)}, u32[]{:S(2)}, u32[]{:S(2)}) collective-permute-start(f32[72,128]{1,0:T(8,128)S(1)} %get-tuple-element.39), channel_id=1, source_target_pairs={{0,16},{8,24},{16,32},{24,40},{32,48},{40,56},{48,0},{56,8},{64,80... | collective-permute-start | bytes 110600 | tf_op jit(solution)/shard_map/ppermute | solution.py:298
  35.0 7.3 %collective-permute-start.5 = (f32[72,128]{1,0:T(8,128)S(1)}, f32[72,128]{1,0:T(8,128)S(1)}, u32[]{:S(2)}, u32[]{:S(2)}) collective-permute-start(f32[72,128]{1,0:T(8,128)S(1)} %get-tuple-element.40), channel_id=1, source_target_pairs={{0,32},{8,40},{16,48},{24,56},{32,0},{40,8},{48,16},{56,24},{64,96... | collective-permute-start | bytes 110600 | tf_op jit(solution)/shard_map/ppermute | solution.py:298
  38.6 4.0 %collective-permute-start.6 = (f32[72,128]{1,0:T(8,128)S(1)}, f32[72,128]{1,0:T(8,128)S(1)}, u32[]{:S(2)}, u32[]{:S(2)}) collective-permute-start(f32[72,128]{1,0:T(8,128)S(1)} %get-tuple-element.41), channel_id=1, source_target_pairs={{0,48},{8,56},{16,0},{24,8},{32,16},{40,24},{48,32},{56,40},{64,11... | collective-permute-start | bytes 110600 | tf_op jit(solution)/shard_map/ppermute | solution.py:298
  39.0 4.0 %collective-permute-start.13 = (f32[72,128]{1,0:T(8,128)S(1)}, f32[72,128]{1,0:T(8,128)S(1)}, u32[]{:S(2)}, u32[]{:S(2)}) collective-permute-start(f32[72,128]{1,0:T(8,128)S(1)} %get-tuple-element.53), channel_id=1, source_target_pairs={{0,64},{8,72},{16,80},{24,88},{32,96},{40,104},{48,112},{56,120},{... | collective-permute-start | bytes 110600 | tf_op jit(solution)/shard_map/ppermute | solution.py:298
  41.2 5.5 %collective-permute-start.14 = (f32[72,128]{1,0:T(8,128)S(1)}, f32[72,128]{1,0:T(8,128)S(1)}, u32[]{:S(2)}, u32[]{:S(2)}) collective-permute-start(f32[72,128]{1,0:T(8,128)S(1)} %get-tuple-element.54), channel_id=1, source_target_pairs={{0,128},{8,136},{16,144},{24,152},{32,160},{40,168},{48,176},{56,1... | collective-permute-start | bytes 110600 | tf_op jit(solution)/shard_map/ppermute | solution.py:298
  42.1 5.2 %collective-permute-start.15 = (f32[72,128]{1,0:T(8,128)S(1)}, f32[72,128]{1,0:T(8,128)S(1)}, u32[]{:S(2)}, u32[]{:S(2)}) collective-permute-start(f32[72,128]{1,0:T(8,128)S(1)} %get-tuple-element.55), channel_id=1, source_target_pairs={{0,192},{8,200},{16,208},{24,216},{32,224},{40,232},{48,240},{56,2... | collective-permute-start | bytes 110600 | tf_op jit(solution)/shard_map/ppermute | solution.py:298
  47.3 5.2 %collective-permute-start.16 = (f32[144,128]{1,0:T(8,128)S(1)}, f32[144,128]{1,0:T(8,128)S(1)}, u32[]{:S(2)}, u32[]{:S(2)}) collective-permute-start(f32[144,128]{1,0:T(8,128)S(1)} %plane.1.total_ref.a_ref), channel_id=1, source_target_pairs={{0,1},{1,0},{2,3},{3,2},{4,5},{5,4},{6,7},{7,6},{8,9},{9,8},{10,11... | collective-permute-start | bytes 221192 | tf_op jit(solution)/shard_map/ppermute | solution.py:342
  52.5 5.3 %collective-permute-start.17 = (f32[144,128]{1,0:T(8,128)S(1)}, f32[144,128]{1,0:T(8,128)S(1)}, u32[]{:S(2)}, u32[]{:S(2)}) collective-permute-start(f32[144,128]{1,0:T(8,128)S(1)} %duo.2.a_ref), channel_id=1, source_target_pairs={{0,2},{1,3},{2,0},{3,1},{4,6},{5,7},{6,4},{7,5},{8,10},{9,11},{10,... | collective-permute-start | bytes 221192 | tf_op jit(solution)/shard_map/ppermute | solution.py:342
  57.9 9.3 %collective-permute-start.18 = (f32[144,128]{1,0:T(8,128)S(1)}, f32[144,128]{1,0:T(8,128)S(1)}, u32[]{:S(2)}, u32[]{:S(2)}) collective-permute-start(f32[144,128]{1,0:T(8,128)S(1)} %duo.3.a_ref), channel_id=1, source_target_pairs={{0,6},{1,7},{2,4},{3,5},{4,2},{5,3},{6,0},{7,1},{8,14},{9,15},{10,... | collective-permute-start | bytes 221192 | tf_op jit(solution)/shard_map/ppermute | solution.py:342

commit v4 on v3

v4 whole, which is shorter than its diff:
```python
import math

import jax
import jax.numpy as jnp
from jax import lax
from jax.experimental import pallas as pl
from jax.experimental.pallas import tpu as pltpu
from jax.sharding import PartitionSpec as P

LAG = 2048
BLK = 1024
LANES = 128
F32 = jnp.float32
CONTRACT = (((0,), (0,)), ((), ()))
VMEM_LIMIT = 47 * 1024 * 1024


def rows_below(limit, shape):
    return lax.broadcasted_iota(jnp.int32, shape, 0) < limit


def keep_below(block, limit):
    wide = jnp.where(rows_below(limit, block.shape), block.astype(F32), 0.0)
    return wide.astype(block.dtype)


def write_chunks(place, acc, tail, keep_ref, send_ref):
    core, my_x, my_y = place[0], place[4], place[5]
    side = keep_ref.shape[0]
    width = acc.shape[1]
    share = acc.shape[0] // (2 * side * side)
    for out, which in ((keep_ref, core), (send_ref, 1 - core)):
        for i in range(side):
            for j in range(side):
                far_x = jnp.where(which == 1, i, j)
                far_y = jnp.where(which == 1, j, i)
                chip = lax.rem(my_x + far_x, side) * side + lax.rem(my_y + far_y, side)
                first = pl.multiple_of((2 * chip + which) * share, share)
                for col in range(width // LANES):
                    out[i, j, col * share : (col + 1) * share, :] = acc[
                        pl.ds(first, share), col * LANES : (col + 1) * LANES
                    ]
                if tail is not None:
                    out[i, j, share * (width // LANES) :, :] = tail


def tail_rows(*sums):
    return jnp.concatenate(
        [each[:, c * LANES : (c + 1) * LANES] for each in sums for c in range(each.shape[1] // LANES)], axis=0
    )


def fold(wide):
    return jnp.sum(wide.reshape(-1, 8, wide.shape[1]), axis=0)


def dot(early, late):
    return lax.dot_general(early, late, CONTRACT, preferred_element_type=F32)


def add_whole(block_ref, first, acc, sums, pair):
    block = block_ref[...]
    acc[...] += dot(block, block)
    if pair is not None:
        pair[0][...] += dot(pair[1][...], block)
    total = fold(block.astype(F32))
    sums[0:8, :] += total
    sums[8:16, :] += total * jnp.where(first >= LAG, 1.0, 0.0)


def add_block(block_ref, first, count, acc, sums, pair):
    full = first + BLK <= count

    @pl.when(full)
    def _():
        add_whole(block_ref, first, acc, sums, pair)

    @pl.when(jnp.logical_and(jnp.logical_not(full), first < count + LAG))
    def _():
        block = block_ref[...]
        wide = block.astype(F32)
        held = jnp.where(rows_below(count - first, wide.shape), wide, 0.0)
        acc[...] += dot(held.astype(block.dtype), block)
        if pair is not None:
            pair[0][...] += dot(keep_below(pair[1][...], count - first + LAG), block)
        later = jnp.where(rows_below(count + LAG - first, wide.shape), wide, 0.0)
        sums[0:8, :] += fold(held)
        sums[8:16, :] += fold(later) * jnp.where(first >= LAG, 1.0, 0.0)


def edges_kernel(place, x_hbm, far_ref, near_ref, sems):
    rows, height = x_hbm.shape[0], far_ref.shape[0]
    parts = sems.shape[0] // 2
    step = height // parts
    copies = []
    for which, out in ((1, far_ref), (0, near_ref)):
        start = jnp.where(place[0] == which, rows - height, 0)
        for k in range(parts):
            source = x_hbm.at[pl.ds(pl.multiple_of(start + k * step, step), step)]
            sem = sems.at[which * parts + k]
            copies.append(pltpu.make_async_copy(source, out.at[pl.ds(k * step, step)], sem))
    for copy in copies:
        copy.start()
    for copy in copies:
        copy.wait()


def moments_kernel(
    place, x_hbm, keep_ref, send_ref, lag, second_ref, late_ref, facts_ref, xs, acc, sums, sems
):
    base, count = place[1], place[2]
    rows = x_hbm.shape[0]
    blocks = rows // BLK
    ahead = LAG // BLK

    def copy(b):
        return pltpu.make_async_copy(x_hbm.at[pl.ds(b * BLK, BLK)], xs.at[b], sems.at[b])

    def again(k, b, out):
        return pltpu.make_async_copy(x_hbm.at[pl.ds(b * BLK, BLK)], out, sems.at[blocks + k])

    kept = [again(0, 1, second_ref), again(1, blocks - ahead, late_ref)]
    for b in range(blocks):
        copy(b).start()
    for each in kept:
        each.start()
    acc[...] = jnp.zeros_like(acc)
    sums[...] = jnp.zeros_like(sums)
    lag[...] = jnp.zeros_like(lag)

    def step(b, with_pair):
        copy(b).wait()
        pair = (lag, xs.at[b - ahead]) if with_pair else None
        add_block(xs.at[b], base + b * BLK, count, acc, sums, pair)

    pl.loop(0, ahead)(lambda b: step(b, False))
    pl.loop(ahead, blocks)(lambda b: step(b, True))
    for each in kept:
        each.wait()
    sum_x = jnp.sum(sums[0:8, :], axis=0, keepdims=True)
    sum_y = jnp.sum(sums[8:16, :], axis=0, keepdims=True)
    write_chunks(place, acc, tail_rows(sum_x, sum_y), keep_ref, send_ref)
    facts_ref[0:8, :] = jnp.full((8, LANES), count, jnp.int32).astype(F32)
    facts_ref[8:16, :] = jnp.full((8, LANES), place[3], jnp.int32).astype(F32)


def border_kernel(
    place, far_ref, near_ref, second_ref, late_ref, part_ref, keep_ref, send_ref, acc
):
    core, base, count = place[0], place[1], place[2]
    rows = place[6]
    first = base + rows - LAG

    def add(next_ref, last_ref):
        full = first + BLK <= count

        @pl.when(full)
        def _():
            acc[...] = (
                part_ref[...] + dot(late_ref[...], next_ref[...]) + dot(last_ref[...], second_ref[...])
            )

        @pl.when(jnp.logical_not(full))
        def _():
            early = keep_below(late_ref[...], count - first)
            before = keep_below(last_ref[...], count - base + BLK)
            acc[...] = part_ref[...] + dot(early, next_ref[...]) + dot(before, second_ref[...])

    @pl.when(core == 1)
    def _():
        add(far_ref, near_ref)

    @pl.when(core == 0)
    def _():
        add(near_ref, far_ref)

    write_chunks(place, acc, None, keep_ref, send_ref)


def pair_kernel(keep_i, met_i, keep_l, met_l, *outs):
    half = keep_i.shape[2]
    for d, out in enumerate(outs):
        out[:, :half, :] = keep_i[d] + met_i[d]
        out[:, half:, :] = keep_l[d] + met_l[d]


def line_kernel(a_ref, b_ref, c_ref, d_ref, *outs):
    for d, out in enumerate(outs):
        out[...] = (a_ref[d] + b_ref[d]) + (c_ref[d] + d_ref[d])


def plane_kernel(facts_ref, a_ref, b_ref, c_ref, d_ref, total_ref):
    height = a_ref.shape[0]
    total_ref[:height, :] = (a_ref[...] + b_ref[...]) + (c_ref[...] + d_ref[...])
    total_ref[height:, :] = facts_ref[0:8, :]


def row_of(rows):
    return jnp.concatenate([rows[c : c + 1, :] for c in range(rows.shape[0])], axis=1)


def centered(total, mean_rows, mean_cols, number, share, out_ref):
    for col in range(out_ref.shape[1] // LANES):
        lanes = slice(col * LANES, (col + 1) * LANES)
        block = total[col * share : (col + 1) * share, :]
        out_ref[:, lanes] = block / number - mean_rows * mean_cols[:, lanes]


def finish(total, facts_ref, inst_ref, lag_ref):
    share, width = inst_ref.shape
    cols = width // LANES
    flat = share * cols
    after = flat + 2 * cols
    number = total[flat + after : flat + after + 1, 0:1]
    mean_x = row_of(total[flat : flat + cols, :]) / number
    mean_y = row_of(total[flat + cols : after, :]) / number
    row = lax.broadcasted_iota(jnp.int32, (share, width), 0)
    col = lax.broadcasted_iota(jnp.int32, (share, width), 1)
    first_row = facts_ref[8:9, 0:1].astype(jnp.int32)
    own = jnp.where(col - row == jnp.broadcast_to(first_row, row.shape), jnp.broadcast_to(mean_x, (share, width)), 0.0)
    mean_rows = jnp.sum(own, axis=1, keepdims=True)
    centered(total[:flat, :], mean_rows, mean_x, number, share, inst_ref)
    centered(total[after : after + flat, :], mean_rows, mean_y, number, share, lag_ref)


def session_kernel(facts_ref, total_ref, inst_ref, lag_ref):
    finish(total_ref[...], facts_ref, inst_ref, lag_ref)


def duo_kernel(a_ref, b_ref, out_ref):
    out_ref[...] = a_ref[...] + b_ref[...]


def pooled_kernel(facts_ref, a_ref, b_ref, inst_ref, lag_ref):
    finish(a_ref[...] + b_ref[...], facts_ref, inst_ref, lag_ref)


def on_device(frames, pair_count):
    local = frames[0]
    rows, width = local.shape
    blocks = rows // BLK
    parts = lax.axis_size("tm")
    sessions = lax.axis_size("group")
    side = math.isqrt(parts // 2)
    share = width // parts
    flat = share * (width // LANES)
    tail = 2 * (width // LANES)
    chunk = 2 * flat + tail
    me = lax.axis_index("tm")
    numbers = [me % 2, me * rows, pair_count[0], me * share, me // (2 * side), (me // 2) % side, rows]
    place = jnp.stack(numbers).astype(jnp.int32)

    smem = pl.BlockSpec(memory_space=pltpu.SMEM)
    vmem = pl.BlockSpec(memory_space=pltpu.VMEM)
    hbm = pl.BlockSpec(memory_space=pl.ANY)
    params = pltpu.CompilerParams(vmem_limit_bytes=VMEM_LIMIT)

    def floats(*shape):
        return jax.ShapeDtypeStruct(shape, F32)

    def call(kernel, name, ins, out_shape, scratch=(), flops=0, moved=0):
        specs = jax.tree.map(lambda _: vmem, out_shape)
        return pl.pallas_call(
            kernel,
            out_shape=out_shape,
            in_specs=[spec for _, spec in ins],
            out_specs=specs,
            scratch_shapes=list(scratch),
            compiler_params=params,
            cost_estimate=pl.CostEstimate(flops=flops, bytes_accessed=moved, transcendentals=0),
            name=name,
        )(*[operand for operand, _ in ins])

    def dma(n):
        return pltpu.SemaphoreType.DMA((n,))

    where, frames_in = (place, smem), (local, hbm)
    edge = jax.ShapeDtypeStruct((BLK, width), local.dtype)
    swap = [(i, i ^ 1) for i in range(parts)]
    cross = [(i, i + 1 if i % 2 else i - 1) for i in range(1, parts - 1)]

    far, near = call(edges_kernel, "edges", [where, frames_in], (edge, edge), [dma(8)], 0, 4 * BLK * width)
    far = lax.ppermute(far, "tm", cross)
    near = lax.ppermute(near, "tm", swap)

    def at(x, y, c):
        return ((x % side) * side + y % side) * 2 + c

    def gather(blocks, stage):
        came = [blocks[0]]
        for d in range(1, side):
            route = []
            for x in range(side):
                for y in range(side):
                    for c in range(2):
                        on_x = c != stage
                        route.append((at(x, y, c), at(x + d * on_x, y + d * (not on_x), c)))
            came.append(lax.ppermute(blocks[d], "tm", route))
        return came

    square = pltpu.VMEM((width, width), F32)
    held = pltpu.VMEM((blocks, BLK, width), local.dtype)
    work = 2 * rows * width * width
    keep_i, send_i, partial, second, late, facts = call(
        moments_kernel,
        "moments",
        [where, frames_in],
        (*[floats(side, side, flat + tail, LANES)] * 2, floats(width, width), edge, edge, floats(16, LANES)),
        [held, square, pltpu.VMEM((16, width), F32), dma(blocks + 2)],
        work * 7 // 4,
        rows * width * 2,
    )
    keep_l, send_l = call(
        border_kernel,
        "border",
        [where, *[(v, vmem) for v in (far, near, second, late, partial)]],
        [floats(side, side, flat, LANES)] * 2,
        [square],
        work // 4,
        rows * width,
    )
    met_i = lax.ppermute(send_i, "tm", swap)
    met_l = lax.ppermute(send_l, "tm", swap)

    def all_vmem(values):
        return [(v, vmem) for v in values]

    both = floats(side, chunk, LANES)
    lines = call(pair_kernel, "pair", all_vmem((keep_i, met_i, keep_l, met_l)), [both] * side)
    cells = call(line_kernel, "line", all_vmem(gather(lines, 0)), [floats(chunk, LANES)] * side)
    whole = floats(chunk + 8, LANES)
    total = call(plane_kernel, "plane", all_vmem((facts, *gather(cells, 1))), whole)
    out = floats(share, width)
    group_instant, group_lagged = call(session_kernel, "session", all_vmem((facts, total)), (out, out))
    for route in (lambda i: i ^ 1, lambda i: i ^ 2, lambda i: (sessions - 2 - (i & -2)) | (i & 1)):
        other = lax.ppermute(total, "group", [(i, route(i)) for i in range(sessions)])
        last = (total, other)
        total = call(duo_kernel, "duo", all_vmem(last), whole)
    pooled_instant, pooled_lagged = call(
        pooled_kernel, "pooled", all_vmem((facts, *last)), (out, out)
    )
    return (group_instant[None], group_lagged[None], pooled_instant, pooled_lagged)


def solution(mesh):
    in_specs = (P("group", "tm", None), P("group"))
    out_specs = (P("group", "tm", None), P("group", "tm", None), P("tm", None), P("tm", None))
    return jax.shard_map(
        on_device, mesh=mesh, in_specs=in_specs, out_specs=out_specs, check_vma=False
    )
```

time: 68.6 us -> 67 us (0.977)
  waiting for transfers between devices: 15.2 us -> 24.3 us
  starting transfers between devices: 32.2 us -> 23.3 us
  Pallas kernels: 19.6 us -> 17.3 us
    ppermute x16 -> x10, waiting for transfers between devices: 7.87 us -> 16.9 us  [the longest x6 13.4 us: gather(): came.append(lax.ppermute(blocks[d], 'tm', route))]
    ppermute x16 -> x10, starting transfers between devices: 21 us -> 12.2 us  [the longest x6 6.81 us: gather(): came.append(lax.ppermute(blocks[d], 'tm', route))]
    pallas_call x13 -> x10, Pallas kernels: 19.6 us -> 17.3 us  [call(): pl.pallas_call(kernel, out_shape=out_shape, in_specs=[spec for _, spec in...]
  transfers between devices with their start and end apart: 19 -> 13, of which waited for: 9 -> 10; matrix products, arithmetic and copies ran while one was open for 0% -> 0% of each run, Pallas kernels for 24% -> 21%
where the time goes in v4:
time: 67 us; the launch traced here: 66.4 us
  waiting for transfers between devices  24.3 us (36%)
  starting transfers between devices  23.3 us (35%)
  Pallas kernels  17.3 us (26%)
  between operations  1.4 us (2%)
    pallas_call x10, Pallas kernels, call(): pl.pallas_call(kernel, out_shape=out_shape, in_specs=[spec for _, spec in...  17.3 us
    ppermute x6, waiting for transfers between devices, gather(): came.append(lax.ppermute(blocks[d], 'tm', route))  13.4 us
    ppermute x3, starting transfers between devices, on_device(): lax.ppermute(total, 'group', [(i, route(i)) for i in range(sessions)])  11.1 us
    ppermute x3, waiting for transfers between devices, on_device(): lax.ppermute(total, 'group', [(i, route(i)) for i in range(sessions)])  7.45 us
    ppermute x6, starting transfers between devices, gather(): came.append(lax.ppermute(blocks[d], 'tm', route))  6.81 us
    ppermute x1, starting transfers between devices, on_device(): far = lax.ppermute(far, 'tm', cross)  4.63 us
    ppermute x1, waiting for transfers between devices, on_device(): met_l = lax.ppermute(send_l, 'tm', swap)  1.89 us
    ppermute x1, waiting for transfers between devices, on_device(): far = lax.ppermute(far, 'tm', cross)  1.57 us
  transfers between devices with their start and end apart: 13, of which 10 were waited for; matrix products, arithmetic and copies ran while one was open for 0% of the time, Pallas kernels for 21%

profile of v4, /device:TPU:6, one launch (start us, length us, event | category | flops | bytes accessed | tf_op | source)
XLA Modules:
  0.0 66.4 jit_solution(17962507741110024841)
XLA Ops:
  1.4 2.1 %edges.1 = (bf16[1024,512]{1,0:T(8,128)(2,1)S(1)}, bf16[1024,512]{1,0:T(8,128)(2,1)S(1)}) custom-call(s32[7]{0:T(128)S(1)} %stack.23.place, bf16[8192,512]{1,0:T(8,128)(2,1)} %bitcast.8), custom_call_target="tpu_custom_call" | custom-call | bytes 2097152 | tf_op jit(solution)/shard_map/edges/pallas_call | solution.py:263
  3.5 4.6 %collective-permute-start.1 = (bf16[1024,512]{1,0:T(8,128)(2,1)S(1)}, bf16[1024,512]{1,0:T(8,128)(2,1)S(1)}, u32[]{:S(2)}, u32[]{:S(2)}) collective-permute-start(bf16[1024,512]{1,0:T(8,128)(2,1)S(1)} %get-tuple-element.29), channel_id=1, source_target_pairs={{8,16},{16,8},{24,32},{32,24},{40,48},{48,40},{56,64},{64,56},{72,... | collective-permute-start | bytes 3145736 | tf_op jit(solution)/shard_map/ppermute | solution.py:283
  8.3 11.3 %moments.1 = (f32[4,4,72,128]{3,2,1,0:T(8,128)S(1)}, f32[4,4,72,128]{3,2,1,0:T(8,128)S(1)}, f32[512,512]{1,0:T(8,128)S(1)}, bf16[1024,512]{1,0:T(8,128)(2,1)S(1)...) custom-call(s32[7]{0:T(128)S(1)} %stack.23.place, bf16[8192,512]{1,0:T(8,128)(2,1)} %bitcast.9), custom_call_target="tpu_custom_call" | custom-call | flops 7516192768 | bytes 8388608 | tf_op jit(solution)/shard_map/moments/pallas_call | solution.py:263
  19.6 0.6 collective-permute-start
  20.2 1.6 %collective-permute-done.1.far_ref = bf16[1024,512]{1,0:T(8,128)(2,1)S(1)} collective-permute-done((bf16[1024,512]{1,0:T(8,128)(2,1)S(1)}, bf16[1024,512]{1,0:T(8,128)(2,1)S(1)}, u32[]{:S(2)}, u32[]{:S(2)}) %collective-permute-start.1) | collective-permute-done | bytes 1048608 | tf_op jit(solution)/shard_map/ppermute | solution.py:283
  21.8 2.0 %border.1 = (f32[4,4,64,128]{3,2,1,0:T(8,128)S(1)}, f32[4,4,64,128]{3,2,1,0:T(8,128)S(1)}) custom-call(s32[7]{0:T(128)S(1)} %stack.23.place, bf16[1024,512]{1,0:T(8,128)(2,1)S(1)} %collective-permute-done.1.far_ref, bf16[1024,512]{1,0:T(8,128)(2,1)S(1)} %collective-permute-done.2.near_ref, bf16[1024,512]{1,0:T(8,128)(2,1)S(1)} %get-tuple-element.31.second_ref, ...), custom_call_target="tpu_custom_call" | custom-call | flops 1073741824 | bytes 4194304 | tf_op jit(solution)/shard_map/border/pallas_call | solution.py:263
  23.9 1.9 %collective-permute-done.3.met_l = f32[4,4,64,128]{3,2,1,0:T(8,128)S(1)} collective-permute-done((f32[4,4,64,128]{3,2,1,0:T(8,128)S(1)}, f32[4,4,64,128]{3,2,1,0:T(8,128)S(1)}, u32[]{:S(2)}, u32[]{:S(2)}) %collective-permute-start.3) | collective-permute-done | bytes 524320 | tf_op jit(solution)/shard_map/ppermute | solution.py:323
  26.0 2.4 %collective-permute-start.5 = (f32[4,136,128]{2,1,0:T(8,128)S(1)}, f32[4,136,128]{2,1,0:T(8,128)S(1)}, u32[]{:S(2)}, u32[]{:S(2)}) collective-permute-start(f32[4,136,128]{2,1,0:T(8,128)S(1)} %get-tuple-element.38), channel_id=1, source_target_pairs={{0,32},{8,136},{16,48},{24,152},{32,0},{40,168},{48,16},{56,184},{... | collective-permute-start | bytes 835592 | tf_op jit(solution)/shard_map/ppermute | solution.py:298
  28.4 1.3 %collective-permute-start.6 = (f32[4,136,128]{2,1,0:T(8,128)S(1)}, f32[4,136,128]{2,1,0:T(8,128)S(1)}, u32[]{:S(2)}, u32[]{:S(2)}) collective-permute-start(f32[4,136,128]{2,1,0:T(8,128)S(1)} %get-tuple-element.39), channel_id=1, source_target_pairs={{0,48},{8,200},{16,0},{24,216},{32,16},{40,232},{48,32},{56,248},{... | collective-permute-start | bytes 835592 | tf_op jit(solution)/shard_map/ppermute | solution.py:298
  29.8 7.0 %collective-permute-done.4.b_ref = f32[4,136,128]{2,1,0:T(8,128)S(1)} collective-permute-done((f32[4,136,128]{2,1,0:T(8,128)S(1)}, f32[4,136,128]{2,1,0:T(8,128)S(1)}, u32[]{:S(2)}, u32[]{:S(2)}) %collective-permute-start.4) | collective-permute-done | bytes 278560 | tf_op jit(solution)/shard_map/ppermute | solution.py:298
  36.8 0.9 %collective-permute-done.6.d_ref = f32[4,136,128]{2,1,0:T(8,128)S(1)} collective-permute-done((f32[4,136,128]{2,1,0:T(8,128)S(1)}, f32[4,136,128]{2,1,0:T(8,128)S(1)}, u32[]{:S(2)}, u32[]{:S(2)}) %collective-permute-start.6) | collective-permute-done | bytes 278560 | tf_op jit(solution)/shard_map/ppermute | solution.py:298
  37.7 0.4 collective-permute-start.7
  38.1 2.6 %collective-permute-start.8 = (f32[136,128]{1,0:T(8,128)S(1)}, f32[136,128]{1,0:T(8,128)S(1)}, u32[]{:S(2)}, u32[]{:S(2)}) collective-permute-start(f32[136,128]{1,0:T(8,128)S(1)} %get-tuple-element.42), channel_id=1, source_target_pairs={{0,128},{8,40},{16,144},{24,56},{32,160},{40,8},{48,176},{56,24},{... | collective-permute-start | bytes 208904 | tf_op jit(solution)/shard_map/ppermute | solution.py:298
  40.7 1.4 %collective-permute-done.7.b_ref = f32[136,128]{1,0:T(8,128)S(1)} collective-permute-done((f32[136,128]{1,0:T(8,128)S(1)}, f32[136,128]{1,0:T(8,128)S(1)}, u32[]{:S(2)}, u32[]{:S(2)}) %collective-permute-start.7) | collective-permute-done | bytes 69664 | tf_op jit(solution)/shard_map/ppermute | solution.py:298
  42.1 1.8 %collective-permute-done.8.c_ref = f32[136,128]{1,0:T(8,128)S(1)} collective-permute-done((f32[136,128]{1,0:T(8,128)S(1)}, f32[136,128]{1,0:T(8,128)S(1)}, u32[]{:S(2)}, u32[]{:S(2)}) %collective-permute-start.8) | collective-permute-done | bytes 69664 | tf_op jit(solution)/shard_map/ppermute | solution.py:298
  43.9 2.3 %collective-permute-done.9.d_ref = f32[136,128]{1,0:T(8,128)S(1)} collective-permute-done((f32[136,128]{1,0:T(8,128)S(1)}, f32[136,128]{1,0:T(8,128)S(1)}, u32[]{:S(2)}, u32[]{:S(2)}) %collective-permute-start.9) | collective-permute-done | bytes 69664 | tf_op jit(solution)/shard_map/ppermute | solution.py:298
  46.2 2.0 %collective-permute-start.10 = (f32[144,128]{1,0:T(8,128)S(1)}, f32[144,128]{1,0:T(8,128)S(1)}, u32[]{:S(2)}, u32[]{:S(2)}) collective-permute-start(f32[144,128]{1,0:T(8,128)S(1)} %plane.1.total_ref.a_ref), channel_id=1, source_target_pairs={{0,1},{1,0},{2,3},{3,2},{4,5},{5,4},{6,7},{7,6},{8,9},{9,8},{10,11... | collective-permute-start | bytes 221192 | tf_op jit(solution)/shard_map/ppermute | solution.py:336
  48.2 2.4 %collective-permute-done.10.b_ref = f32[144,128]{1,0:T(8,128)S(1)} collective-permute-done((f32[144,128]{1,0:T(8,128)S(1)}, f32[144,128]{1,0:T(8,128)S(1)}, u32[]{:S(2)}, u32[]{:S(2)}) %collective-permute-start.10) | collective-permute-done | bytes 73760 | tf_op jit(solution)/shard_map/ppermute | solution.py:336
  50.7 4.1 %collective-permute-start.11 = (f32[144,128]{1,0:T(8,128)S(1)}, f32[144,128]{1,0:T(8,128)S(1)}, u32[]{:S(2)}, u32[]{:S(2)}) collective-permute-start(f32[144,128]{1,0:T(8,128)S(1)} %duo.2.a_ref), channel_id=1, source_target_pairs={{0,2},{1,3},{2,0},{3,1},{4,6},{5,7},{6,4},{7,5},{8,10},{9,11},{10,... | collective-permute-start | bytes 221192 | tf_op jit(solution)/shard_map/ppermute | solution.py:336
  54.8 3.1 %collective-permute-done.11.b_ref = f32[144,128]{1,0:T(8,128)S(1)} collective-permute-done((f32[144,128]{1,0:T(8,128)S(1)}, f32[144,128]{1,0:T(8,128)S(1)}, u32[]{:S(2)}, u32[]{:S(2)}) %collective-permute-start.11) | collective-permute-done | bytes 73760 | tf_op jit(solution)/shard_map/ppermute | solution.py:336
  57.9 5.0 %collective-permute-start.12 = (f32[144,128]{1,0:T(8,128)S(1)}, f32[144,128]{1,0:T(8,128)S(1)}, u32[]{:S(2)}, u32[]{:S(2)}) collective-permute-start(f32[144,128]{1,0:T(8,128)S(1)} %duo.3.a_ref), channel_id=1, source_target_pairs={{0,6},{1,7},{2,4},{3,5},{4,2},{5,3},{6,0},{7,1},{8,14},{9,15},{10,... | collective-permute-start | bytes 221192 | tf_op jit(solution)/shard_map/ppermute | solution.py:336
  62.9 0.8 %session.1 = (f32[16,512]{1,0:T(8,128)}, f32[16,512]{1,0:T(8,128)}) custom-call(f32[16,128]{1,0:T(8,128)S(1)} %get-tuple-element.26.facts_ref, f32[144,128]{1,0:T(8,128)S(1)} %plane.1.total_ref.a_ref), custom_call_target="tpu_custom_call" | custom-call | tf_op jit(solution)/shard_map/session/pallas_call | solution.py:263
  63.7 1.9 %collective-permute-done.12.b_ref = f32[144,128]{1,0:T(8,128)S(1)} collective-permute-done((f32[144,128]{1,0:T(8,128)S(1)}, f32[144,128]{1,0:T(8,128)S(1)}, u32[]{:S(2)}, u32[]{:S(2)}) %collective-permute-start.12) | collective-permute-done | bytes 73760 | tf_op jit(solution)/shard_map/ppermute | solution.py:336
  65.6 0.8 %pooled.1 = (f32[16,512]{1,0:T(8,128)}, f32[16,512]{1,0:T(8,128)}) custom-call(f32[16,128]{1,0:T(8,128)S(1)} %get-tuple-element.26.facts_ref, f32[144,128]{1,0:T(8,128)S(1)} %duo.3.a_ref, f32[144,128]{1,0:T(8,128)S(1)} %collective-permute-done.12.b_ref), custom_call_target="tpu_custom_call" | custom-call | tf_op jit(solution)/shard_map/pooled/pallas_call | solution.py:263
  (13 shorter events, 0.6 us)
Async XLA Ops:
  3.5 18.2 %collective-permute-start.1 = (bf16[1024,512]{1,0:T(8,128)(2,1)S(1)}, bf16[1024,512]{1,0:T(8,128)(2,1)S(1)}, u32[]{:S(2)}, u32[]{:S(2)}) collective-permute-start(bf16[1024,512]{1,0:T(8,128)(2,1)S(1)} %get-tuple-element.29), channel_id=1, source_target_pairs={{8,16},{16,8},{24,32},{32,24},{40,48},{48,40},{56,64},{64,56},{72,... | collective-permute-start | bytes 3145736 | tf_op jit(solution)/shard_map/ppermute | solution.py:283
  8.2 13.6 %collective-permute-start.2 = (bf16[1024,512]{1,0:T(8,128)(2,1)S(1)}, bf16[1024,512]{1,0:T(8,128)(2,1)S(1)}, u32[]{:S(2)}, u32[]{:S(2)}) collective-permute-start(bf16[1024,512]{1,0:T(8,128)(2,1)S(1)} %get-tuple-element.30), channel_id=1, source_target_pairs={{0,8},{8,0},{16,24},{24,16},{32,40},{40,32},{48,56},{56,48},{64,72... | collective-permute-start | bytes 3145736 | tf_op jit(solution)/shard_map/ppermute | solution.py:284
  19.6 4.3 %collective-permute-start = (f32[4,4,72,128]{3,2,1,0:T(8,128)S(1)}, f32[4,4,72,128]{3,2,1,0:T(8,128)S(1)}, u32[]{:S(2)}, u32[]{:S(2)}) collective-permute-start(f32[4,4,72,128]{3,2,1,0:T(8,128)S(1)} %get-tuple-element.28), channel_id=1, source_target_pairs={{0,8},{8,0},{16,24},{24,16},{32,40},{40,32},{48,56},{56,48},{64,72... | collective-permute-start | bytes 1769480 | tf_op jit(solution)/shard_map/ppermute | solution.py:322
  23.8 2.0 %collective-permute-start.3 = (f32[4,4,64,128]{3,2,1,0:T(8,128)S(1)}, f32[4,4,64,128]{3,2,1,0:T(8,128)S(1)}, u32[]{:S(2)}, u32[]{:S(2)}) collective-permute-start(f32[4,4,64,128]{3,2,1,0:T(8,128)S(1)} %get-tuple-element.35), channel_id=1, source_target_pairs={{0,8},{8,0},{16,24},{24,16},{32,40},{40,32},{48,56},{56,48},{64,72... | collective-permute-start | bytes 1572872 | tf_op jit(solution)/shard_map/ppermute | solution.py:323
  25.9 10.8 %collective-permute-start.4 = (f32[4,136,128]{2,1,0:T(8,128)S(1)}, f32[4,136,128]{2,1,0:T(8,128)S(1)}, u32[]{:S(2)}, u32[]{:S(2)}) collective-permute-start(f32[4,136,128]{2,1,0:T(8,128)S(1)} %get-tuple-element.37), channel_id=1, source_target_pairs={{0,16},{8,72},{16,32},{24,88},{32,48},{40,104},{48,0},{56,120},{64... | collective-permute-start | bytes 835592 | tf_op jit(solution)/shard_map/ppermute | solution.py:298
  26.0 10.7 %collective-permute-start.5 = (f32[4,136,128]{2,1,0:T(8,128)S(1)}, f32[4,136,128]{2,1,0:T(8,128)S(1)}, u32[]{:S(2)}, u32[]{:S(2)}) collective-permute-start(f32[4,136,128]{2,1,0:T(8,128)S(1)} %get-tuple-element.38), channel_id=1, source_target_pairs={{0,32},{8,136},{16,48},{24,152},{32,0},{40,168},{48,16},{56,184},{... | collective-permute-start | bytes 835592 | tf_op jit(solution)/shard_map/ppermute | solution.py:298
  28.4 9.2 %collective-permute-start.6 = (f32[4,136,128]{2,1,0:T(8,128)S(1)}, f32[4,136,128]{2,1,0:T(8,128)S(1)}, u32[]{:S(2)}, u32[]{:S(2)}) collective-permute-start(f32[4,136,128]{2,1,0:T(8,128)S(1)} %get-tuple-element.39), channel_id=1, source_target_pairs={{0,48},{8,200},{16,0},{24,216},{32,16},{40,232},{48,32},{56,248},{... | collective-permute-start | bytes 835592 | tf_op jit(solution)/shard_map/ppermute | solution.py:298
  37.7 4.4 %collective-permute-start.7 = (f32[136,128]{1,0:T(8,128)S(1)}, f32[136,128]{1,0:T(8,128)S(1)}, u32[]{:S(2)}, u32[]{:S(2)}) collective-permute-start(f32[136,128]{1,0:T(8,128)S(1)} %get-tuple-element.41), channel_id=1, source_target_pairs={{0,64},{8,24},{16,80},{24,40},{32,96},{40,56},{48,112},{56,8},{64,... | collective-permute-start | bytes 208904 | tf_op jit(solution)/shard_map/ppermute | solution.py:298
  38.1 5.8 %collective-permute-start.8 = (f32[136,128]{1,0:T(8,128)S(1)}, f32[136,128]{1,0:T(8,128)S(1)}, u32[]{:S(2)}, u32[]{:S(2)}) collective-permute-start(f32[136,128]{1,0:T(8,128)S(1)} %get-tuple-element.42), channel_id=1, source_target_pairs={{0,128},{8,40},{16,144},{24,56},{32,160},{40,8},{48,176},{56,24},{... | collective-permute-start | bytes 208904 | tf_op jit(solution)/shard_map/ppermute | solution.py:298
  40.7 5.5 %collective-permute-start.9 = (f32[136,128]{1,0:T(8,128)S(1)}, f32[136,128]{1,0:T(8,128)S(1)}, u32[]{:S(2)}, u32[]{:S(2)}) collective-permute-start(f32[136,128]{1,0:T(8,128)S(1)} %get-tuple-element.43), channel_id=1, source_target_pairs={{0,192},{8,56},{16,208},{24,8},{32,224},{40,24},{48,240},{56,40},{... | collective-permute-start | bytes 208904 | tf_op jit(solution)/shard_map/ppermute | solution.py:298
  46.2 4.4 %collective-permute-start.10 = (f32[144,128]{1,0:T(8,128)S(1)}, f32[144,128]{1,0:T(8,128)S(1)}, u32[]{:S(2)}, u32[]{:S(2)}) collective-permute-start(f32[144,128]{1,0:T(8,128)S(1)} %plane.1.total_ref.a_ref), channel_id=1, source_target_pairs={{0,1},{1,0},{2,3},{3,2},{4,5},{5,4},{6,7},{7,6},{8,9},{9,8},{10,11... | collective-permute-start | bytes 221192 | tf_op jit(solution)/shard_map/ppermute | solution.py:336
  50.7 7.2 %collective-permute-start.11 = (f32[144,128]{1,0:T(8,128)S(1)}, f32[144,128]{1,0:T(8,128)S(1)}, u32[]{:S(2)}, u32[]{:S(2)}) collective-permute-start(f32[144,128]{1,0:T(8,128)S(1)} %duo.2.a_ref), channel_id=1, source_target_pairs={{0,2},{1,3},{2,0},{3,1},{4,6},{5,7},{6,4},{7,5},{8,10},{9,11},{10,... | collective-permute-start | bytes 221192 | tf_op jit(solution)/shard_map/ppermute | solution.py:336
  57.9 7.7 %collective-permute-start.12 = (f32[144,128]{1,0:T(8,128)S(1)}, f32[144,128]{1,0:T(8,128)S(1)}, u32[]{:S(2)}, u32[]{:S(2)}) collective-permute-start(f32[144,128]{1,0:T(8,128)S(1)} %duo.3.a_ref), channel_id=1, source_target_pairs={{0,6},{1,7},{2,4},{3,5},{4,2},{5,3},{6,0},{7,1},{8,14},{9,15},{10,... | collective-permute-start | bytes 221192 | tf_op jit(solution)/shard_map/ppermute | solution.py:336

commit v5 on v4

--- a/solution.py
+++ b/solution.py
@@ -1,3 +1,4 @@
+import functools
 import math
 
 import jax
@@ -144,37 +145,31 @@
     facts_ref[8:16, :] = jnp.full((8, LANES), place[3], jnp.int32).astype(F32)
 
 
-def border_kernel(
-    place, far_ref, near_ref, second_ref, late_ref, part_ref, keep_ref, send_ref, acc
-):
+def border_kernel(far, place, met_ref, second_ref, late_ref, part_ref, *outs):
     core, base, count = place[0], place[1], place[2]
-    rows = place[6]
-    first = base + rows - LAG
-
-    def add(next_ref, last_ref):
+    total = outs[-1]
+
+    def add(first, early_ref, late_ref):
         full = first + BLK <= count
 
         @pl.when(full)
         def _():
-            acc[...] = (
-                part_ref[...] + dot(late_ref[...], next_ref[...]) + dot(last_ref[...], second_ref[...])
-            )
+            total[...] = part_ref[...] + dot(early_ref[...], late_ref[...])
 
         @pl.when(jnp.logical_not(full))
         def _():
-            early = keep_below(late_ref[...], count - first)
-            before = keep_below(last_ref[...], count - base + BLK)
-            acc[...] = part_ref[...] + dot(early, next_ref[...]) + dot(before, second_ref[...])
-
-    @pl.when(core == 1)
+            total[...] = part_ref[...] + dot(keep_below(early_ref[...], count - first), late_ref[...])
+
+    @pl.when(core == far)
     def _():
-        add(far_ref, near_ref)
-
-    @pl.when(core == 0)
+        add(base + place[6] - LAG, late_ref, met_ref)
+
+    @pl.when(core != far)
     def _():
-        add(near_ref, far_ref)
-
-    write_chunks(place, acc, None, keep_ref, send_ref)
+        add(base - BLK, met_ref, second_ref)
+
+    if far:
+        write_chunks(place, total, None, outs[0], outs[1])
 
 
 def pair_kernel(keep_i, met_i, keep_l, met_l, *outs):
@@ -310,13 +305,22 @@
         work * 7 // 4,
         rows * width * 2,
     )
+    partial = call(
+        functools.partial(border_kernel, 0),
+        "border_near",
+        [where, *[(v, vmem) for v in (near, second, late, partial)]],
+        floats(width, width),
+        (),
+        work // 8,
+        rows * width,
+    )
     keep_l, send_l = call(
-        border_kernel,
-        "border",
-        [where, *[(v, vmem) for v in (far, near, second, late, partial)]],
+        functools.partial(border_kernel, 1),
+        "border_far",
+        [where, *[(v, vmem) for v in (far, second, late, partial)]],
         [floats(side, side, flat, LANES)] * 2,
         [square],
-        work // 4,
+        work // 8,
         rows * width,
     )
     met_i = lax.ppermute(send_i, "tm", swap)

time: 67 us -> 66.5 us (level)
  Pallas kernels: 17.3 us -> 11.6 us
  waiting for transfers between devices: 24.3 us -> 28.6 us
  starting transfers between devices: 23.3 us -> 24.7 us
    pallas_call x10 -> x11, Pallas kernels: 17.3 us -> 11.6 us  [call(): pl.pallas_call(kernel, out_shape=out_shape, in_specs=[spec for _, spec in...]
    ppermute x1, waiting for transfers between devices: 1.57 us -> 6.67 us  [on_device(): far = lax.ppermute(far, 'tm', cross)]
    ppermute x3, waiting for transfers between devices: 7.45 us -> 6.68 us  [on_device(): lax.ppermute(total, 'group', [(i, route(i)) for i in range(sessions)])]
    ppermute x3, starting transfers between devices: 11.1 us -> 11.8 us  [on_device(): lax.ppermute(total, 'group', [(i, route(i)) for i in range(sessions)])]
  transfers between devices with their start and end apart: 13 -> 13, of which waited for: 10 -> 10; matrix products, arithmetic and copies ran while one was open for 0% -> 0% of each run, Pallas kernels for 21% -> 13%
where the time goes in v5:
time: 66.5 us; the launch traced here: 66.3 us
  waiting for transfers between devices  28.6 us (43%)
  starting transfers between devices  24.7 us (37%)
  Pallas kernels  11.6 us (17%)
  between operations  1.43 us (2%)
    ppermute x6, waiting for transfers between devices, gather(): came.append(lax.ppermute(blocks[d], 'tm', route))  13.3 us
    ppermute x3, starting transfers between devices, on_device(): lax.ppermute(total, 'group', [(i, route(i)) for i in range(sessions)])  11.8 us
    pallas_call x11, Pallas kernels, call(): pl.pallas_call(kernel, out_shape=out_shape, in_specs=[spec for _, spec in...  11.6 us
    ppermute x6, starting transfers between devices, gather(): came.append(lax.ppermute(blocks[d], 'tm', route))  7.31 us
    ppermute x3, waiting for transfers between devices, on_device(): lax.ppermute(total, 'group', [(i, route(i)) for i in range(sessions)])  6.68 us
    ppermute x1, waiting for transfers between devices, on_device(): far = lax.ppermute(far, 'tm', cross)  6.67 us
    ppermute x1, starting transfers between devices, on_device(): far = lax.ppermute(far, 'tm', cross)  5.28 us
    ppermute x1, waiting for transfers between devices, on_device(): met_l = lax.ppermute(send_l, 'tm', swap)  1.89 us
  transfers between devices with their start and end apart: 13, of which 10 were waited for; matrix products, arithmetic and copies ran while one was open for 0% of the time, Pallas kernels for 13%

profile of v5, /device:TPU:6, one launch (start us, length us, event | category | flops | bytes accessed | tf_op | source)
XLA Modules:
  0.0 66.3 jit_solution(6361496725752677464)
XLA Ops:
  1.4 2.1 %edges.1 = (bf16[1024,512]{1,0:T(8,128)(2,1)S(1)}, bf16[1024,512]{1,0:T(8,128)(2,1)S(1)}) custom-call(s32[7]{0:T(128)S(1)} %stack.23.place, bf16[8192,512]{1,0:T(8,128)(2,1)} %bitcast.8), custom_call_target="tpu_custom_call" | custom-call | bytes 2097152 | tf_op jit(solution)/shard_map/edges/pallas_call | solution.py:258
  3.6 5.3 %collective-permute-start.1 = (bf16[1024,512]{1,0:T(8,128)(2,1)S(1)}, bf16[1024,512]{1,0:T(8,128)(2,1)S(1)}, u32[]{:S(2)}, u32[]{:S(2)}) collective-permute-start(bf16[1024,512]{1,0:T(8,128)(2,1)S(1)} %get-tuple-element.29), channel_id=1, source_target_pairs={{8,16},{16,8},{24,32},{32,24},{40,48},{48,40},{56,64},{64,56},{72,... | collective-permute-start | bytes 3145736 | tf_op jit(solution)/shard_map/ppermute | solution.py:278
  8.9 4.8 %moments.1 = (f32[4,4,72,128]{3,2,1,0:T(8,128)S(1)}, f32[4,4,72,128]{3,2,1,0:T(8,128)S(1)}, f32[512,512]{1,0:T(8,128)S(1)}, bf16[1024,512]{1,0:T(8,128)(2,1)S(1)...) custom-call(s32[7]{0:T(128)S(1)} %stack.23.place, bf16[8192,512]{1,0:T(8,128)(2,1)} %bitcast.9), custom_call_target="tpu_custom_call" | custom-call | flops 7516192768 | bytes 8388608 | tf_op jit(solution)/shard_map/moments/pallas_call | solution.py:258
  13.9 1.3 %border_near.1.part_ref = f32[512,512]{1,0:T(8,128)S(1)} custom-call(s32[7]{0:T(128)S(1)} %stack.23.place, bf16[1024,512]{1,0:T(8,128)(2,1)S(1)} %collective-permute-done.2.met_ref, bf16[1024,512]{1,0:T(8,128)(2,1)S(1)} %get-tuple-element.30.second_ref, bf16[1024,512]{1,0:T(8,128)(2,1)S(1)} %get-tuple-element.31.late_ref, ...), custom_call_target="tpu_custom_call" | custom-call | flops 536870912 | bytes 4194304 | tf_op jit(solution)/shard_map/border_near/pallas_call | solution.py:258
  15.2 6.7 %collective-permute-done.1.met_ref = bf16[1024,512]{1,0:T(8,128)(2,1)S(1)} collective-permute-done((bf16[1024,512]{1,0:T(8,128)(2,1)S(1)}, bf16[1024,512]{1,0:T(8,128)(2,1)S(1)}, u32[]{:S(2)}, u32[]{:S(2)}) %collective-permute-start.1) | collective-permute-done | bytes 1048608 | tf_op jit(solution)/shard_map/ppermute | solution.py:278
  21.9 1.5 %border_far.1 = (f32[4,4,64,128]{3,2,1,0:T(8,128)S(1)}, f32[4,4,64,128]{3,2,1,0:T(8,128)S(1)}) custom-call(s32[7]{0:T(128)S(1)} %stack.23.place, bf16[1024,512]{1,0:T(8,128)(2,1)S(1)} %collective-permute-done.1.met_ref, bf16[1024,512]{1,0:T(8,128)(2,1)S(1)} %get-tuple-element.30.second_ref, bf16[1024,512]{1,0:T(8,128)(2,1)S(1)} %get-tuple-element.31.late_ref, ...), custom_call_target="tpu_custom_call" | custom-call | flops 536870912 | bytes 4194304 | tf_op jit(solution)/shard_map/border_far/pallas_call | solution.py:258
  23.5 1.9 %collective-permute-done.3.met_l = f32[4,4,64,128]{3,2,1,0:T(8,128)S(1)} collective-permute-done((f32[4,4,64,128]{3,2,1,0:T(8,128)S(1)}, f32[4,4,64,128]{3,2,1,0:T(8,128)S(1)}, u32[]{:S(2)}, u32[]{:S(2)}) %collective-permute-start.3) | collective-permute-done | bytes 524320 | tf_op jit(solution)/shard_map/ppermute | solution.py:327
  25.6 2.4 %collective-permute-start.5 = (f32[4,136,128]{2,1,0:T(8,128)S(1)}, f32[4,136,128]{2,1,0:T(8,128)S(1)}, u32[]{:S(2)}, u32[]{:S(2)}) collective-permute-start(f32[4,136,128]{2,1,0:T(8,128)S(1)} %get-tuple-element.38), channel_id=1, source_target_pairs={{0,32},{8,136},{16,48},{24,152},{32,0},{40,168},{48,16},{56,184},{... | collective-permute-start | bytes 835592 | tf_op jit(solution)/shard_map/ppermute | solution.py:293
  28.0 1.5 %collective-permute-start.6 = (f32[4,136,128]{2,1,0:T(8,128)S(1)}, f32[4,136,128]{2,1,0:T(8,128)S(1)}, u32[]{:S(2)}, u32[]{:S(2)}) collective-permute-start(f32[4,136,128]{2,1,0:T(8,128)S(1)} %get-tuple-element.39), channel_id=1, source_target_pairs={{0,48},{8,200},{16,0},{24,216},{32,16},{40,232},{48,32},{56,248},{... | collective-permute-start | bytes 835592 | tf_op jit(solution)/shard_map/ppermute | solution.py:293
  29.4 6.9 %collective-permute-done.4.b_ref = f32[4,136,128]{2,1,0:T(8,128)S(1)} collective-permute-done((f32[4,136,128]{2,1,0:T(8,128)S(1)}, f32[4,136,128]{2,1,0:T(8,128)S(1)}, u32[]{:S(2)}, u32[]{:S(2)}) %collective-permute-start.4) | collective-permute-done | bytes 278560 | tf_op jit(solution)/shard_map/ppermute | solution.py:293
  36.3 0.9 %collective-permute-done.6.d_ref = f32[4,136,128]{2,1,0:T(8,128)S(1)} collective-permute-done((f32[4,136,128]{2,1,0:T(8,128)S(1)}, f32[4,136,128]{2,1,0:T(8,128)S(1)}, u32[]{:S(2)}, u32[]{:S(2)}) %collective-permute-start.6) | collective-permute-done | bytes 278560 | tf_op jit(solution)/shard_map/ppermute | solution.py:293
  37.3 1.0 %collective-permute-start.7 = (f32[136,128]{1,0:T(8,128)S(1)}, f32[136,128]{1,0:T(8,128)S(1)}, u32[]{:S(2)}, u32[]{:S(2)}) collective-permute-start(f32[136,128]{1,0:T(8,128)S(1)} %get-tuple-element.41), channel_id=1, source_target_pairs={{0,64},{8,24},{16,80},{24,40},{32,96},{40,56},{48,112},{56,8},{64,... | collective-permute-start | bytes 208904 | tf_op jit(solution)/shard_map/ppermute | solution.py:293
  38.3 2.4 %collective-permute-start.8 = (f32[136,128]{1,0:T(8,128)S(1)}, f32[136,128]{1,0:T(8,128)S(1)}, u32[]{:S(2)}, u32[]{:S(2)}) collective-permute-start(f32[136,128]{1,0:T(8,128)S(1)} %get-tuple-element.42), channel_id=1, source_target_pairs={{0,128},{8,40},{16,144},{24,56},{32,160},{40,8},{48,176},{56,24},{... | collective-permute-start | bytes 208904 | tf_op jit(solution)/shard_map/ppermute | solution.py:293
  40.7 1.0 %collective-permute-done.7.b_ref = f32[136,128]{1,0:T(8,128)S(1)} collective-permute-done((f32[136,128]{1,0:T(8,128)S(1)}, f32[136,128]{1,0:T(8,128)S(1)}, u32[]{:S(2)}, u32[]{:S(2)}) %collective-permute-start.7) | collective-permute-done | bytes 69664 | tf_op jit(solution)/shard_map/ppermute | solution.py:293
  41.7 2.4 %collective-permute-done.8.c_ref = f32[136,128]{1,0:T(8,128)S(1)} collective-permute-done((f32[136,128]{1,0:T(8,128)S(1)}, f32[136,128]{1,0:T(8,128)S(1)}, u32[]{:S(2)}, u32[]{:S(2)}) %collective-permute-start.8) | collective-permute-done | bytes 69664 | tf_op jit(solution)/shard_map/ppermute | solution.py:293
  44.1 2.1 %collective-permute-done.9.d_ref = f32[136,128]{1,0:T(8,128)S(1)} collective-permute-done((f32[136,128]{1,0:T(8,128)S(1)}, f32[136,128]{1,0:T(8,128)S(1)}, u32[]{:S(2)}, u32[]{:S(2)}) %collective-permute-start.9) | collective-permute-done | bytes 69664 | tf_op jit(solution)/shard_map/ppermute | solution.py:293
  46.2 2.0 %collective-permute-start.10 = (f32[144,128]{1,0:T(8,128)S(1)}, f32[144,128]{1,0:T(8,128)S(1)}, u32[]{:S(2)}, u32[]{:S(2)}) collective-permute-start(f32[144,128]{1,0:T(8,128)S(1)} %plane.1.total_ref.a_ref), channel_id=1, source_target_pairs={{0,1},{1,0},{2,3},{3,2},{4,5},{5,4},{6,7},{7,6},{8,9},{9,8},{10,11... | collective-permute-start | bytes 221192 | tf_op jit(solution)/shard_map/ppermute | solution.py:340
  48.2 2.4 %collective-permute-done.10.b_ref = f32[144,128]{1,0:T(8,128)S(1)} collective-permute-done((f32[144,128]{1,0:T(8,128)S(1)}, f32[144,128]{1,0:T(8,128)S(1)}, u32[]{:S(2)}, u32[]{:S(2)}) %collective-permute-start.10) | collective-permute-done | bytes 73760 | tf_op jit(solution)/shard_map/ppermute | solution.py:340
  50.7 3.9 %collective-permute-start.11 = (f32[144,128]{1,0:T(8,128)S(1)}, f32[144,128]{1,0:T(8,128)S(1)}, u32[]{:S(2)}, u32[]{:S(2)}) collective-permute-start(f32[144,128]{1,0:T(8,128)S(1)} %duo.2.a_ref), channel_id=1, source_target_pairs={{0,2},{1,3},{2,0},{3,1},{4,6},{5,7},{6,4},{7,5},{8,10},{9,11},{10,... | collective-permute-start | bytes 221192 | tf_op jit(solution)/shard_map/ppermute | solution.py:340
  54.6 2.3 %collective-permute-done.11.b_ref = f32[144,128]{1,0:T(8,128)S(1)} collective-permute-done((f32[144,128]{1,0:T(8,128)S(1)}, f32[144,128]{1,0:T(8,128)S(1)}, u32[]{:S(2)}, u32[]{:S(2)}) %collective-permute-start.11) | collective-permute-done | bytes 73760 | tf_op jit(solution)/shard_map/ppermute | solution.py:340
  56.9 5.9 %collective-permute-start.12 = (f32[144,128]{1,0:T(8,128)S(1)}, f32[144,128]{1,0:T(8,128)S(1)}, u32[]{:S(2)}, u32[]{:S(2)}) collective-permute-start(f32[144,128]{1,0:T(8,128)S(1)} %duo.3.a_ref), channel_id=1, source_target_pairs={{0,6},{1,7},{2,4},{3,5},{4,2},{5,3},{6,0},{7,1},{8,14},{9,15},{10,... | collective-permute-start | bytes 221192 | tf_op jit(solution)/shard_map/ppermute | solution.py:340
  62.9 0.8 %session.1 = (f32[16,512]{1,0:T(8,128)}, f32[16,512]{1,0:T(8,128)}) custom-call(f32[16,128]{1,0:T(8,128)S(1)} %get-tuple-element.26.facts_ref, f32[144,128]{1,0:T(8,128)S(1)} %plane.1.total_ref.a_ref), custom_call_target="tpu_custom_call" | custom-call | tf_op jit(solution)/shard_map/session/pallas_call | solution.py:258
  63.6 1.9 %collective-permute-done.12.b_ref = f32[144,128]{1,0:T(8,128)S(1)} collective-permute-done((f32[144,128]{1,0:T(8,128)S(1)}, f32[144,128]{1,0:T(8,128)S(1)}, u32[]{:S(2)}, u32[]{:S(2)}) %collective-permute-start.12) | collective-permute-done | bytes 73760 | tf_op jit(solution)/shard_map/ppermute | solution.py:340
  65.6 0.8 %pooled.1 = (f32[16,512]{1,0:T(8,128)}, f32[16,512]{1,0:T(8,128)}) custom-call(f32[16,128]{1,0:T(8,128)S(1)} %get-tuple-element.26.facts_ref, f32[144,128]{1,0:T(8,128)S(1)} %duo.3.a_ref, f32[144,128]{1,0:T(8,128)S(1)} %collective-permute-done.12.b_ref), custom_call_target="tpu_custom_call" | custom-call | tf_op jit(solution)/shard_map/pooled/pallas_call | solution.py:258
  (14 shorter events, 0.7 us)
Async XLA Ops:
  3.5 10.3 %collective-permute-start.2 = (bf16[1024,512]{1,0:T(8,128)(2,1)S(1)}, bf16[1024,512]{1,0:T(8,128)(2,1)S(1)}, u32[]{:S(2)}, u32[]{:S(2)}) collective-permute-start(bf16[1024,512]{1,0:T(8,128)(2,1)S(1)} %get-tuple-element.32), channel_id=1, source_target_pairs={{0,8},{8,0},{16,24},{24,16},{32,40},{40,32},{48,56},{56,48},{64,72... | collective-permute-start | bytes 3145736 | tf_op jit(solution)/shard_map/ppermute | solution.py:279
  3.6 18.2 %collective-permute-start.1 = (bf16[1024,512]{1,0:T(8,128)(2,1)S(1)}, bf16[1024,512]{1,0:T(8,128)(2,1)S(1)}, u32[]{:S(2)}, u32[]{:S(2)}) collective-permute-start(bf16[1024,512]{1,0:T(8,128)(2,1)S(1)} %get-tuple-element.29), channel_id=1, source_target_pairs={{8,16},{16,8},{24,32},{32,24},{40,48},{48,40},{56,64},{64,56},{72,... | collective-permute-start | bytes 3145736 | tf_op jit(solution)/shard_map/ppermute | solution.py:278
  13.7 9.7 %collective-permute-start = (f32[4,4,72,128]{3,2,1,0:T(8,128)S(1)}, f32[4,4,72,128]{3,2,1,0:T(8,128)S(1)}, u32[]{:S(2)}, u32[]{:S(2)}) collective-permute-start(f32[4,4,72,128]{3,2,1,0:T(8,128)S(1)} %get-tuple-element.28), channel_id=1, source_target_pairs={{0,8},{8,0},{16,24},{24,16},{32,40},{40,32},{48,56},{56,48},{64,72... | collective-permute-start | bytes 1769480 | tf_op jit(solution)/shard_map/ppermute | solution.py:326
  23.4 2.0 %collective-permute-start.3 = (f32[4,4,64,128]{3,2,1,0:T(8,128)S(1)}, f32[4,4,64,128]{3,2,1,0:T(8,128)S(1)}, u32[]{:S(2)}, u32[]{:S(2)}) collective-permute-start(f32[4,4,64,128]{3,2,1,0:T(8,128)S(1)} %get-tuple-element.35), channel_id=1, source_target_pairs={{0,8},{8,0},{16,24},{24,16},{32,40},{40,32},{48,56},{56,48},{64,72... | collective-permute-start | bytes 1572872 | tf_op jit(solution)/shard_map/ppermute | solution.py:327
  25.5 10.8 %collective-permute-start.4 = (f32[4,136,128]{2,1,0:T(8,128)S(1)}, f32[4,136,128]{2,1,0:T(8,128)S(1)}, u32[]{:S(2)}, u32[]{:S(2)}) collective-permute-start(f32[4,136,128]{2,1,0:T(8,128)S(1)} %get-tuple-element.37), channel_id=1, source_target_pairs={{0,16},{8,72},{16,32},{24,88},{32,48},{40,104},{48,0},{56,120},{64... | collective-permute-start | bytes 835592 | tf_op jit(solution)/shard_map/ppermute | solution.py:293
  25.6 10.7 %collective-permute-start.5 = (f32[4,136,128]{2,1,0:T(8,128)S(1)}, f32[4,136,128]{2,1,0:T(8,128)S(1)}, u32[]{:S(2)}, u32[]{:S(2)}) collective-permute-start(f32[4,136,128]{2,1,0:T(8,128)S(1)} %get-tuple-element.38), channel_id=1, source_target_pairs={{0,32},{8,136},{16,48},{24,152},{32,0},{40,168},{48,16},{56,184},{... | collective-permute-start | bytes 835592 | tf_op jit(solution)/shard_map/ppermute | solution.py:293
  28.0 9.3 %collective-permute-start.6 = (f32[4,136,128]{2,1,0:T(8,128)S(1)}, f32[4,136,128]{2,1,0:T(8,128)S(1)}, u32[]{:S(2)}, u32[]{:S(2)}) collective-permute-start(f32[4,136,128]{2,1,0:T(8,128)S(1)} %get-tuple-element.39), channel_id=1, source_target_pairs={{0,48},{8,200},{16,0},{24,216},{32,16},{40,232},{48,32},{56,248},{... | collective-permute-start | bytes 835592 | tf_op jit(solution)/shard_map/ppermute | solution.py:293
  37.3 4.4 %collective-permute-start.7 = (f32[136,128]{1,0:T(8,128)S(1)}, f32[136,128]{1,0:T(8,128)S(1)}, u32[]{:S(2)}, u32[]{:S(2)}) collective-permute-start(f32[136,128]{1,0:T(8,128)S(1)} %get-tuple-element.41), channel_id=1, source_target_pairs={{0,64},{8,24},{16,80},{24,40},{32,96},{40,56},{48,112},{56,8},{64,... | collective-permute-start | bytes 208904 | tf_op jit(solution)/shard_map/ppermute | solution.py:293
  38.3 5.8 %collective-permute-start.8 = (f32[136,128]{1,0:T(8,128)S(1)}, f32[136,128]{1,0:T(8,128)S(1)}, u32[]{:S(2)}, u32[]{:S(2)}) collective-permute-start(f32[136,128]{1,0:T(8,128)S(1)} %get-tuple-element.42), channel_id=1, source_target_pairs={{0,128},{8,40},{16,144},{24,56},{32,160},{40,8},{48,176},{56,24},{... | collective-permute-start | bytes 208904 | tf_op jit(solution)/shard_map/ppermute | solution.py:293
  40.7 5.5 %collective-permute-start.9 = (f32[136,128]{1,0:T(8,128)S(1)}, f32[136,128]{1,0:T(8,128)S(1)}, u32[]{:S(2)}, u32[]{:S(2)}) collective-permute-start(f32[136,128]{1,0:T(8,128)S(1)} %get-tuple-element.43), channel_id=1, source_target_pairs={{0,192},{8,56},{16,208},{24,8},{32,224},{40,24},{48,240},{56,40},{... | collective-permute-start | bytes 208904 | tf_op jit(solution)/shard_map/ppermute | solution.py:293
  46.2 4.4 %collective-permute-start.10 = (f32[144,128]{1,0:T(8,128)S(1)}, f32[144,128]{1,0:T(8,128)S(1)}, u32[]{:S(2)}, u32[]{:S(2)}) collective-permute-start(f32[144,128]{1,0:T(8,128)S(1)} %plane.1.total_ref.a_ref), channel_id=1, source_target_pairs={{0,1},{1,0},{2,3},{3,2},{4,5},{5,4},{6,7},{7,6},{8,9},{9,8},{10,11... | collective-permute-start | bytes 221192 | tf_op jit(solution)/shard_map/ppermute | solution.py:340
  50.7 6.2 %collective-permute-start.11 = (f32[144,128]{1,0:T(8,128)S(1)}, f32[144,128]{1,0:T(8,128)S(1)}, u32[]{:S(2)}, u32[]{:S(2)}) collective-permute-start(f32[144,128]{1,0:T(8,128)S(1)} %duo.2.a_ref), channel_id=1, source_target_pairs={{0,2},{1,3},{2,0},{3,1},{4,6},{5,7},{6,4},{7,5},{8,10},{9,11},{10,... | collective-permute-start | bytes 221192 | tf_op jit(solution)/shard_map/ppermute | solution.py:340
  56.9 8.6 %collective-permute-start.12 = (f32[144,128]{1,0:T(8,128)S(1)}, f32[144,128]{1,0:T(8,128)S(1)}, u32[]{:S(2)}, u32[]{:S(2)}) collective-permute-start(f32[144,128]{1,0:T(8,128)S(1)} %duo.3.a_ref), channel_id=1, source_target_pairs={{0,6},{1,7},{2,4},{3,5},{4,2},{5,3},{6,0},{7,1},{8,14},{9,15},{10,... | collective-permute-start | bytes 221192 | tf_op jit(solution)/shard_map/ppermute | solution.py:340
